TPU v7x, 512 devices: a whole 4x4x16 slice. The times are simulated.
512 devices in a mesh: sensor: 8 (over y, core), tm: 64 (over z, x).
Axes of the slice: x: 4, y: 4, z: 16, core: 2. Of those that a mesh axis runs over, the one named last changes fastest.
Arguments:
- recording: bfloat16 [256, 65536], P('sensor', 'tm'), may hold values from -6 to 6
- spatial_w: bfloat16 [512, 256], P(None, 'sensor'), may hold values from -0.375 to 0.375
- conv_w: bfloat16 [3, 3, 512, 512], P(None, None, 'sensor'), may hold values from -0.15625 to 0.15625
- conv_b: float32 [3, 512], P(None, 'sensor'), may hold values from -3 to 3
- dilations: int32 [3], replicated, may hold values from 1 to 16, as said below
- valid_frames: int32 [64], P('tm'), may hold values from 512 to 1024, as said below
- key_w: bfloat16 [512, 512], P('sensor'), may hold values from -0.25 to 0.25
- value_w: bfloat16 [512, 512], P('sensor'), may hold values from -0.25 to 0.25
- queries: bfloat16 [512, 2048], P('sensor'), may hold values from -60 to 60
Outputs:
- features: bfloat16 [512, 65536], P('sensor', 'tm')
- attended: bfloat16 [512, 2048], P('sensor')
Inputs may be any that keep to these rules, and one draw needn't show every extreme that they name: `dilations`: one layer has dilation exactly 16 and another exactly 1. `valid_frames`: one block is full and one holds exactly half of its 1024 frames.
All inputs are finite; a program needn't handle non-finite values.
Results may differ from a plain program's by a relative error of at most 0.015.
The roundings to bfloat16 on the way count: a program that leaves them out, or rounds other values in their place, can miss the bound.
Values may be sent and summed in bfloat16 or wider, within the bound.
A program may use at most 64 MiB of HBM per device.

v0:
```python
import math

import jax
import jax.numpy as jnp
from jax import lax
from jax.sharding import PartitionSpec as P

HD = 64
LATENTS = 2048
LAYERS = 3
DMAX = 16


def padded_2(cells, sides, width):
    for axis, dim in sides:
        count = lax.axis_size(axis)
        ends = count - 1
        head = lax.slice_in_dim(cells, 0, width, axis=dim)
        tail = lax.slice_in_dim(cells, cells.shape[dim] - width, cells.shape[dim], axis=dim)
        cells = jnp.concatenate(
            [
                lax.ppermute(tail, axis, [(i, (i + 1) % count) for i in range(ends)]),
                cells,
                lax.ppermute(head, axis, [((i + 1) % count, i) for i in range(ends)]),
            ],
            axis=dim,
        )
    return cells


def tap_folder(kernels, dilation, frames):

    def add_taps(running, portion, first_row):
        for tap_index in range(3):
            kernel = kernels[tap_index]
            offset = DMAX + (tap_index - 1) * dilation
            shifted = lax.dynamic_slice_in_dim(portion, offset, frames, 1)
            running = running + jnp.dot(kernel, shifted, preferred_element_type=jnp.float32)
        return running

    return add_taps


def on_device(
    recording, spatial_w, conv_w, conv_b, dilations, valid_frames, key_w, value_w, queries
):
    frames = recording.shape[1]
    ch_loc = conv_w.shape[2]
    hidden = lax.psum_scatter(
        jnp.dot(spatial_w, recording, preferred_element_type=jnp.float32),
        "sensor",
        scatter_dimension=0,
        tiled=True,
    ).astype(jnp.bfloat16)
    for layer in range(LAYERS):
        padded = padded_2(hidden, (("tm", 1),), DMAX)
        initial = jnp.broadcast_to(conv_b[layer][:, None], (ch_loc, frames))
        folder = tap_folder(conv_w[layer], dilations[layer], frames)
        preact = folder(initial, lax.all_gather(padded, "sensor", axis=0, tiled=True), jnp.int32(0))
        hidden = (hidden.astype(jnp.float32) + jax.nn.gelu(preact, approximate=False)).astype(
            jnp.bfloat16
        )
    portion = lax.all_gather(hidden, "sensor", axis=0, tiled=True)
    key_rows = jnp.dot(key_w, portion, preferred_element_type=jnp.float32)
    value_rows = jnp.dot(value_w, portion, preferred_element_type=jnp.float32)
    head_count = key_w.shape[0] // HD
    key_heads = key_rows.astype(jnp.bfloat16).reshape(head_count, HD, frames)
    value_heads = value_rows.astype(jnp.bfloat16).reshape(head_count, HD, frames)
    frame_mask = jnp.arange(frames, dtype=jnp.int32) < valid_frames[0]
    block_rows = min(LATENTS, 512)
    block_count = LATENTS // block_rows
    query_blocks = queries.reshape(head_count, HD, block_count, block_rows).transpose(2, 0, 1, 3)
    scale = 1.0 / math.sqrt(HD)

    def attend(query_block):
        scores = (
            jnp.einsum("hdq,hdt->hqt", query_block, key_heads, preferred_element_type=jnp.float32)
            * scale
        )
        scores = jnp.where(frame_mask[None, None, :], scores, -jnp.inf)
        peaks = jnp.max(scores, axis=2)
        probs = jnp.where(frame_mask[None, None, :], jnp.exp(scores - peaks[:, :, None]), 0.0)
        totals = jnp.sum(probs, axis=2)
        weighted = jnp.einsum(
            "hqt,hdt->hdq",
            probs.astype(jnp.bfloat16),
            value_heads,
            preferred_element_type=jnp.float32,
        )
        return (peaks, totals, weighted)

    peaks, totals, weighted = lax.map(attend, query_blocks)
    peaks = peaks.transpose(1, 0, 2).reshape(head_count, LATENTS)
    totals = totals.transpose(1, 0, 2).reshape(head_count, LATENTS)
    weighted = weighted.transpose(1, 2, 0, 3).reshape(head_count, HD, LATENTS)
    global_peaks = lax.pmax(peaks, "tm")
    rescale = jnp.exp(peaks - global_peaks)
    totals, weighted = lax.psum((totals * rescale, weighted * rescale[:, None, :]), "tm")
    attended = (
        (weighted / totals[:, None, :]).reshape(head_count * HD, LATENTS).astype(jnp.bfloat16)
    )
    return (hidden, attended)


def solution(mesh):
    return jax.shard_map(
        on_device,
        mesh=mesh,
        in_specs=(
            P("sensor", "tm"),
            P(None, "sensor"),
            P(None, None, "sensor", None),
            P(None, "sensor"),
            P(),
            P("tm"),
            P("sensor", None),
            P("sensor", None),
            P("sensor", None),
        ),
        out_specs=(P("sensor", "tm"), P("sensor", None)),
        check_vma=False,
    )
```

profile of v0, /device:TPU:6, one launch (start us, length us, event | category | flops | bytes accessed | tf_op | source)
XLA Modules:
  0.0 660.8 jit_solution(14581788557916473280)
XLA Ops:
  7.2 0.0 reduce-scatter.2.cloned.1.call-start
  7.3 0.8 copy-done
  8.0 2.5 fusion.136
  10.6 0.0 all-gather.5.cloned.1.call-start
  10.6 45.9 %reduce-scatter.2.cloned.1.call-done = f32[64,1024]{1,0:T(8,128)} async-done(((f32[512,1024]{1,0:T(8,128)}), f32[64,1024]{1,0:T(8,128)}) %reduce-scatter.2.cloned.1.call-update) | async-done | bytes 262160 | tf_op jit(solution)/shard_map/reduce_scatter | solution.py:49
  56.6 1.0 convert_element_type.43
  57.5 0.1 fusion.134
  57.6 3.5 collective-permute-start
  61.1 2.3 collective-permute-start.1
  63.5 5.4 collective-permute-done.1
  68.9 0.8 concatenate.9
  69.7 0.0 all-gather.7.cloned.1.call-start
  69.8 0.7 fusion.135
  72.4 27.6 %all-gather.5.cloned.1.call-done = bf16[512,1056]{1,0:T(8,128)(2,1)} async-done(((bf16[64,1056]{1,0:T(8,128)(2,1)}), bf16[512,1056]{1,0:T(8,128)(2,1)}) %all-gather.5.cloned.1.call-update) | async-done | bytes 1081360 | tf_op jit(solution)/shard_map/all_gather | solution.py:59
  100.0 1.9 fusion.32
  101.9 1.8 fusion.40
  103.7 1.1 fusion.46
  104.8 0.1 fusion.133
  104.8 3.4 collective-permute-start.2
  108.3 2.4 collective-permute-start.3
  110.7 5.3 collective-permute-done.3
  116.0 0.8 concatenate.10
  116.9 0.0 all-gather.9.cloned.1.call-start
  118.8 29.6 %all-gather.7.cloned.1.call-done = bf16[512,1056]{1,0:T(8,128)(2,1)} async-done(((bf16[64,1056]{1,0:T(8,128)(2,1)}), bf16[512,1056]{1,0:T(8,128)(2,1)}) %all-gather.7.cloned.1.call-update) | async-done | bytes 1081360 | tf_op jit(solution)/shard_map/all_gather | solution.py:59
  148.4 1.9 fusion.30
  150.3 1.8 fusion.37
  152.1 1.1 fusion.50
  153.2 0.1 fusion.132
  153.3 3.4 collective-permute-start.4
  156.7 2.4 collective-permute-start.5
  159.1 5.3 collective-permute-done.5
  164.4 0.8 concatenate.11
  165.3 0.0 all-gather.11.cloned.1.call-start
  167.3 29.5 %all-gather.9.cloned.1.call-done = bf16[512,1056]{1,0:T(8,128)(2,1)} async-done(((bf16[64,1056]{1,0:T(8,128)(2,1)}), bf16[512,1056]{1,0:T(8,128)(2,1)}) %all-gather.9.cloned.1.call-update) | async-done | bytes 1081360 | tf_op jit(solution)/shard_map/all_gather | solution.py:59
  196.8 1.9 fusion.28
  198.7 1.8 fusion.34
  200.5 1.7 fusion.54
  202.3 0.0 all-reduce.2.cloned.1.call-start
  202.4 0.2 reshape.143
  202.6 31.0 %all-gather.11.cloned.1.call-done = bf16[512,1024]{1,0:T(8,128)(2,1)} async-done(((bf16[64,1024]{1,0:T(8,128)(2,1)}), bf16[512,1024]{1,0:T(8,128)(2,1)}) %all-gather.11.cloned.1.call-update) | async-done | bytes 1048592 | tf_op jit(solution)/shard_map/all_gather | solution.py:63
  233.6 1.5 fusion.26
  235.2 1.5 fusion.27
  236.7 10.1 %while.15 = (s32[]{:T(128)}, f32[4,1,512]{2,1,0:T(1,128)S(1)}, f32[4,1,512]{2,1,0:T(1,128)S(1)}, f32[4,1,64,512]{3,2,1,0:T(8,128)S(1)}, bf16[4,1,64,512]{3,2,1,0...) while((s32[]{:T(128)}, f32[4,1,512]{2,1,0:T(1,128)S(1)}, ...), condition=%wide.region_4.5_spmd.clone, body=%wide.region_1.4_spmd.clone.sunk | while | flops 141033472 | bytes 6770797 | solution.py:92
  236.7 0.7 iota_compare_fusion.2
  237.4 0.6 fusion.150
  237.9 0.7 fusion.152
  238.6 0.6 fusion.151
  239.2 0.7 iota_compare_fusion.2
  239.9 0.5 fusion.150
  240.5 0.7 fusion.152
  241.1 0.6 fusion.151
  241.8 0.7 iota_compare_fusion.2
  242.4 0.5 fusion.150
  243.0 0.7 fusion.152
  243.6 0.6 fusion.151
  244.3 0.7 iota_compare_fusion.2
  245.0 0.5 fusion.150
  245.5 0.7 fusion.152
  246.2 0.6 fusion.151
  246.8 138.3 %pmax.7 = f32[1,2048]{1,0:T(1,128)S(1)} all-reduce(f32[1,2048]{1,0:T(1,128)S(1)} %bitcast.298), channel_id=1, replica_groups=mesh['sensor'=8,'tm'=64] {'tm'}, use_global_device_ids=true, to_apply=%region_5.6 | all-reduce | flops 2048 | bytes 16384 | tf_op jit(solution)/shard_map/pmax | solution.py:96
  385.2 0.8 broadcast_multiply_fusion
  386.1 144.7 %psum.15 = f32[2048]{0:T(1024)S(1)} all-reduce(f32[2048]{0:T(1024)S(1)} %bitcast.300), channel_id=1, replica_groups=mesh['sensor'=8,'tm'=64] {'tm'}, use_global_device_ids=true, to_apply=%region_7.8 | all-reduce | flops 2048 | bytes 16384 | tf_op jit(solution)/shard_map/psum | solution.py:98
  530.8 121.4 %all-reduce.2.cloned.1.call-done = f32[1,64,2048]{2,1,0:T(8,128)} async-done(((f32[1,64,2048]{2,1,0:T(8,128)}), f32[1,64,2048]{2,1,0:T(8,128)}) %all-reduce.2.cloned.1.call-update) | async-done | bytes 524304 | tf_op jit(solution)/shard_map/psum | solution.py:98
  652.2 1.8 fusion.94
  (39 shorter events, 0.3 us)
Async XLA Ops:
  7.2 0.8 copy-start
  7.2 62.6 %copy-start.8 = (s32[3]{0:T(128)S(1)}, s32[3]{0:T(128)}, u32[]{:S(2)}) copy-start(s32[3]{0:T(128)} %param.15) | copy-start | bytes 40
  7.2 65.2 %copy-start.9 = (f32[3,64]{1,0:T(4,128)S(1)}, f32[3,64]{1,0:T(4,128)}, u32[]{:S(2)}) copy-start(f32[3,64]{1,0:T(4,128)} %param.14) | copy-start | bytes 2308
  7.2 92.8 %copy-start.5 = (bf16[3,3,64,512]{3,2,1,0:T(8,128)(2,1)S(1)}, bf16[3,3,64,512]{3,2,1,0:T(8,128)(2,1)}, u32[]{:S(2)}) copy-start(bf16[3,3,64,512]{3,2,1,0:T(8,128)(2,1)} %param.13) | copy-start | bytes 1769476
  7.2 49.4 %reduce-scatter.2.cloned.1.call-start = ((), (), s32[]{:S(2)}) async-start(), calls=%async_computation.1 | async-start | bytes 2359296 | tf_op jit(solution)/shard_map/reduce_scatter | solution.py:49
  10.6 89.4 %all-gather.5.cloned.1.call-start = ((), (), s32[]{:S(2)}) async-start(), calls=%async_computation.2 | async-start | bytes 1327104 | tf_op jit(solution)/shard_map/all_gather | solution.py:59
  57.6 5.8 collective-permute-start
  61.1 7.7 %collective-permute-start.1 = (bf16[64,16]{1,0:T(8,128)(2,1)S(1)}, bf16[64,16]{1,0:T(8,128)(2,1)S(1)}, u32[]{:S(2)}, u32[]{:S(2)}) collective-permute-start(bf16[64,16]{1,0:T(8,128)(2,1)S(1)} %get-tuple-element.102), channel_id=1, source_target_pairs={{1,0},{2,1},{3,2},{4,3},{5,4},{6,5},{7,6},{8,7},{9,8},{10,9},{11,1... | collective-permute-start | bytes 6152 | tf_op jit(solution)/shard_map/ppermute | solution.py:24
  69.7 78.7 %all-gather.7.cloned.1.call-start = ((), (), s32[]{:S(2)}) async-start(), calls=%async_computation.3 | async-start | bytes 1327104 | tf_op jit(solution)/shard_map/all_gather | solution.py:59
  100.0 3.7 copy-start.1
  104.8 5.8 collective-permute-start.2
  108.3 7.7 %collective-permute-start.3 = (bf16[64,16]{1,0:T(8,128)(2,1)S(1)}, bf16[64,16]{1,0:T(8,128)(2,1)S(1)}, u32[]{:S(2)}, u32[]{:S(2)}) collective-permute-start(bf16[64,16]{1,0:T(8,128)(2,1)S(1)} %get-tuple-element.100), channel_id=1, source_target_pairs={{1,0},{2,1},{3,2},{4,3},{5,4},{6,5},{7,6},{8,7},{9,8},{10,9},{11,1... | collective-permute-start | bytes 6152 | tf_op jit(solution)/shard_map/ppermute | solution.py:24
  116.9 80.0 %all-gather.9.cloned.1.call-start = ((), (), s32[]{:S(2)}) async-start(), calls=%async_computation.4 | async-start | bytes 1327104 | tf_op jit(solution)/shard_map/all_gather | solution.py:59
  148.4 3.7 copy-start.3
  153.3 5.8 collective-permute-start.4
  156.7 7.7 %collective-permute-start.5 = (bf16[64,16]{1,0:T(8,128)(2,1)S(1)}, bf16[64,16]{1,0:T(8,128)(2,1)S(1)}, u32[]{:S(2)}, u32[]{:S(2)}) collective-permute-start(bf16[64,16]{1,0:T(8,128)(2,1)S(1)} %get-tuple-element.98), channel_id=1, source_target_pairs={{1,0},{2,1},{3,2},{4,3},{5,4},{6,5},{7,6},{8,7},{9,8},{10,9},{11,1... | collective-permute-start | bytes 6152 | tf_op jit(solution)/shard_map/ppermute | solution.py:24
  165.3 68.3 %all-gather.11.cloned.1.call-start = ((), (), s32[]{:S(2)}) async-start(), calls=%async_computation.5 | async-start | bytes 1179648 | tf_op jit(solution)/shard_map/all_gather | solution.py:63
  196.8 3.7 copy-start.2
  200.5 1.9 copy-start.4
  200.5 33.1 %copy-start.6 = (bf16[64,512]{1,0:T(8,128)(2,1)S(1)}, bf16[64,512]{1,0:T(8,128)(2,1)}, u32[]{:S(2)}) copy-start(bf16[64,512]{1,0:T(8,128)(2,1)} %param.17) | copy-start | bytes 196612
  202.3 32.9 %copy-start.7 = (bf16[64,512]{1,0:T(8,128)(2,1)S(1)}, bf16[64,512]{1,0:T(8,128)(2,1)}, u32[]{:S(2)}) copy-start(bf16[64,512]{1,0:T(8,128)(2,1)} %param.18) | copy-start | bytes 196612
  202.3 449.9 %all-reduce.2.cloned.1.call-start = ((), (), s32[]{:S(2)}) async-start(), calls=%async_computation.6 | async-start | bytes 1048576 | tf_op jit(solution)/shard_map/psum | solution.py:98
Sparse Core Ops, SparseCore 0:
  10.9 45.6 reduce-scatter.1
  69.8 30.1 all-gather.4
  117.0 31.3 all-gather.6
  165.4 31.3 all-gather.8
  202.4 31.1 all-gather.10
  386.2 265.9 all-reduce.1
where the time goes:
time: 663 us; the launch traced here: 661 us
  waiting for transfers between devices  301 us (45%)
  blocking collectives  283 us (43%)
  matrix products  25.2 us (4%)
  between operations  20.2 us (3%)
  starting transfers between devices  17.7 us (3%)
  other arithmetic  8.78 us (1%)
    psum x1, blocking collectives, on_device(): lax.psum((totals * rescale, weighted * rescale[:, None, :]), 'tm')  145 us
    pmax x1, blocking collectives, on_device(): global_peaks = lax.pmax(peaks, 'tm')  138 us
    psum x1, waiting for transfers between devices, on_device(): lax.psum((totals * rescale, weighted * rescale[:, None, :]), 'tm')  121 us
    all_gather x3, waiting for transfers between devices, on_device(): lax.all_gather(padded, 'sensor', axis=0, tiled=True)  86.8 us
    reduce_scatter x1, waiting for transfers between devices, on_device(): lax.psum_scatter(jnp.dot(spatial_w, recording, preferred_element_type=jnp...  45.9 us
    all_gather x1, waiting for transfers between devices, on_device(): portion = lax.all_gather(hidden, 'sensor', axis=0, tiled=True)  31 us
    ppermute x3, waiting for transfers between devices, padded_2(): lax.ppermute(head, axis, [((i + 1) % count, i) for i in range(ends)])  16.1 us
    dot_general x9, matrix products, add_taps(): jnp.dot(kernel, shifted, preferred_element_type=jnp.float32)  14.8 us
  transfers between devices with their start and end apart: 12, of which 9 were waited for; matrix products, arithmetic and copies ran while one was open for 0% of the time, Pallas kernels for 0%

commit v1 on v0

v1 whole, which is shorter than its diff:
```python
import jax
import jax.numpy as jnp
from jax import lax
from jax.experimental import pallas as pl
from jax.experimental.pallas import tpu as pltpu
from jax.sharding import PartitionSpec as P

MESH = pl.DeviceIdType.MESH
BF16 = jnp.bfloat16
F32 = jnp.float32
NY, NX, NZ = 4, 4, 16
HD = 64
LATENTS = 2048
QUARTER = 512
LB = 256


def dot(a, b):
    return jnp.dot(a, b, preferred_element_type=F32)


def kernel(
    dil_ref, valid_ref, rec_ref, sw_ref, cw_ref, cb_ref, kw_ref, vw_ref, q_ref,
    feat_ref, att_ref,
    swt, st, sfull, rec, wc, bias, kvw, h0, h1, h2, h3, taps, resid, kv, kvall, ka, kt, va, qa,
    xsend, xlse_send, xrecv, xlse, zsend, zlse_send, zrecv, zlse,
    st_s, st_r, rec_s, rec_r, w_s, w_r, loc, g_s, g_r, kv_s, kv_r, f_s, f_r,
    xs, xr, xls, xlr, zs, zr, zls, zlr, as_, ar, bs, br,
):
    s = lax.axis_index("sensor")
    t = lax.axis_index("tm")
    y, c = s // 2, lax.rem(s, 2)
    z, x = t // NX, lax.rem(t, NX)
    other = 1 - c

    def at_y(i, core):
        return (lax.rem(y + i, NY) * 2 + core, t)

    sibling = (y * 2 + other, t)
    prev_tm = lax.rem(t + 63, 64)
    next_tm = lax.rem(t + 1, 64)

    def at_x(i):
        return (s, z * NX + lax.rem(x + i, NX))

    def at_z(i):
        return (s, lax.rem(z + i, NZ) * NX + x)

    barrier = pltpu.get_barrier_semaphore()

    def greet(device):
        pl.semaphore_signal(barrier, inc=1, device_id=device, device_id_type=MESH)

    for i in range(NY):
        for core in range(2):
            greet((i * 2 + core, jnp.where(c == 0, prev_tm, next_tm)))
    for i in range(1, NY):
        greet(at_y(i, c))
        greet(at_y(i, other))
    greet(sibling)
    for i in range(1, NX):
        greet(at_x(i))

    def greet_z(i, carry):
        greet(at_z(i))
        return carry

    lax.fori_loop(1, NZ, greet_z, 0)

    swt[...] = jnp.transpose(sw_ref[...].astype(F32)).astype(BF16)
    bias[c] = jnp.zeros((8, 128), F32)
    bias[c, 0:3, 0:64] = cb_ref[...]
    own_rows = pl.ds(pl.multiple_of(32 * s, 32), 32)
    st[own_rows, :] = swt[...]

    pl.semaphore_wait(barrier, 8 + 7 + 3 + 15)

    def remote(src, dst, ssem, rsem, device):
        copy = pltpu.make_async_remote_copy(
            src_ref=src, dst_ref=dst, send_sem=ssem, recv_sem=rsem,
            device_id=device, device_id_type=MESH,
        )
        copy.start()
        return copy

    rec_copies = []
    st_copies = []
    peers = [(i, k) for i in range(1, NY) for k in range(2)] + [(0, 1)]
    for n, (i, k) in enumerate(peers):
        core = lax.rem(c + k, 2)
        device = at_y(i, core)
        st_copies.append(remote(swt, st.at[own_rows], st_s.at[n], st_r.at[n], device))
        src = rec_ref.at[:, pl.ds(pl.multiple_of(384 * core, 128), 640)]
        dst = rec.at[own_rows, pl.ds(pl.multiple_of(128 - 128 * core, 128), 640)]
        rec_copies.append(remote(src, dst, rec_s.at[n], rec_r.at[n], device))
    for i in range(NY):
        rec_copies.append(
            remote(
                rec_ref.at[:, 896:1024], rec.at[own_rows, 0:128],
                rec_s.at[7 + i], rec_r.at[7 + 2 * i + c],
                (lax.rem(y + i, NY) * 2, next_tm),
            )
        )
        rec_copies.append(
            remote(
                rec_ref.at[:, 0:128], rec.at[own_rows, 640:768],
                rec_s.at[11 + i], rec_r.at[7 + 2 * i + c],
                (lax.rem(y + i, NY) * 2 + 1, prev_tm),
            )
        )
    own_w = pl.ds(pl.multiple_of(64 * c, 64), 64)
    own_k = pl.ds(pl.multiple_of(128 * c, 64), 64)
    own_v = pl.ds(pl.multiple_of(128 * c + 64, 64), 64)
    w_copies = [
        remote(cw_ref, wc.at[:, :, own_w, :], w_s.at[0], w_r.at[0], sibling),
        remote(kw_ref, kvw.at[own_k], w_s.at[1], w_r.at[1], sibling),
        remote(vw_ref, kvw.at[own_v], w_s.at[2], w_r.at[2], sibling),
        remote(bias.at[c], bias.at[c], w_s.at[3], w_r.at[3], sibling),
    ]
    local = [
        pltpu.make_async_copy(cw_ref, wc.at[:, :, own_w, :], loc.at[0]),
        pltpu.make_async_copy(kw_ref, kvw.at[own_k], loc.at[1]),
        pltpu.make_async_copy(vw_ref, kvw.at[own_v], loc.at[2]),
        pltpu.make_async_copy(
            rec_ref.at[:, pl.ds(pl.multiple_of(384 * c, 128), 640)],
            rec.at[own_rows, pl.ds(pl.multiple_of(128 - 128 * c, 128), 640)],
            loc.at[3],
        ),
    ]
    for copy in local:
        copy.start()
    qa[0:64, :] = q_ref[...]
    first = lax.broadcasted_iota(jnp.int32, (64, LATENTS), 0) == 0
    qa[64:128, :] = jnp.where(first, 1.0, 0.0).astype(BF16)
    va[64:80, :] = jnp.ones((16, 1024), BF16)
    frame = lax.broadcasted_iota(jnp.int32, (64, 1024), 1)
    row = lax.broadcasted_iota(jnp.int32, (64, 1024), 0)
    ka[64:128, :] = jnp.where((row == 0) & (frame >= valid_ref[0]), -1e30, 0.0).astype(BF16)

    for copy in st_copies:
        copy.wait()
    sfull[...] = jnp.transpose(st[...].astype(F32)).astype(BF16)
    for copy in local:
        copy.wait()
    for copy in rec_copies[:7]:
        copy.wait()
    for n, copy in enumerate(rec_copies[7:]):
        copy.wait_send()
    for n in range(8):
        pltpu.make_async_copy(rec_ref.at[:, 0:128], rec.at[0:32, 0:128], rec_r.at[7 + n]).wait()

    low = jnp.where((t == 0) & (c == 0), 0, -4096)
    high = jnp.where((t == 63) & (c == 1), 512, 4096)

    def inside(rows, lanes, start):
        f = lax.broadcasted_iota(jnp.int32, (rows, lanes), 1) + start
        return (f >= low) & (f < high)

    for n in range(0, 768, 256):
        part = dot(sfull[...], rec[:, n : n + 256])
        h0[:, n : n + 256] = jnp.where(inside(512, 256, n - 128), part, 0.0).astype(BF16)

    for copy in w_copies:
        copy.wait()
    both_bias = jnp.transpose(
        jnp.concatenate([bias[0][:, 0:64], bias[1][:, 0:64]], axis=1)
    )

    def shifted(ref, rows, tiles, amount):
        lane = lax.broadcasted_iota(jnp.int32, (128, 128), 1)
        keep = lane < 128 - amount
        turn = lax.rem(128 - amount, 128)
        last = ref.shape[1] // 128 - 1
        rolled = [
            pltpu.roll(ref[rows, 128 * k : 128 * k + 128], turn, 1)
            for k in range(min(tiles, last) + 1)
        ]
        return [jnp.where(keep, rolled[k], rolled[min(k + 1, last)]) for k in range(tiles)]

    chip_rows = pl.ds(pl.multiple_of(128 * y, 128), 128)

    def conv(layer, source, target, width, offset, tiles, start):
        w = wc[layer].reshape(384, 512)
        for n in range(0, width, 256):
            size = min(256, width - n)
            taps[:, n : n + size] = dot(w, source[:, n : n + size])
        resid[:, 0:width] = source[chip_rows, :].astype(F32)
        d = dil_ref[layer]
        view = taps.at[:, 0:width]
        a = shifted(view, slice(0, 128), tiles, offset - d)
        b = shifted(view, slice(128, 256), tiles, jnp.int32(offset))
        e = shifted(view, slice(256, 384), tiles, offset + d)
        r = shifted(resid.at[:, 0:width], slice(0, 128), tiles, jnp.int32(offset))
        col = both_bias[:, layer : layer + 1]
        for k in range(tiles):
            pre = col + a[k] + b[k] + e[k]
            out = r[k] + 0.5 * pre * (1.0 + lax.erf(pre * 0.7071067811865476))
            out = jnp.where(inside(128, 128, start + 128 * k), out, 0.0)
            target[chip_rows, 128 * k : 128 * k + 128] = out.astype(BF16)
        return [
            remote(
                target.at[chip_rows], target.at[chip_rows],
                g_s.at[3 * layer + i - 1], g_r.at[3 * layer + i - 1], at_y(i, c),
            )
            for i in range(1, NY)
        ]

    for copy in conv(0, h0, h1, 768, 64, 5, -64):
        copy.wait()
    for copy in conv(1, h1, h2, 640, 16, 5, -48):
        copy.wait()
    gather = conv(2, h2, h3, 640, 48, 4, 0)
    half = pl.ds(pl.multiple_of(512 * c, 512), 512)
    feature_copy = remote(
        h3.at[pl.ds(pl.multiple_of(128 * y + 64 * other, 64), 64)], feat_ref.at[:, half],
        f_s, f_r, sibling,
    )
    feat_ref[:, half] = h3[pl.ds(pl.multiple_of(128 * y + 64 * c, 64), 64), :]
    for copy in gather:
        copy.wait()

    for n in range(0, 512, 256):
        kv[:, n : n + 256] = dot(kvw[...], h3[:, n : n + 256]).astype(BF16)
    kv_copy = remote(
        kv.at[pl.ds(pl.multiple_of(128 * other, 128), 128)], kvall.at[:, half], kv_s, kv_r, sibling
    )
    kvall[:, half] = kv[pl.ds(pl.multiple_of(128 * c, 128), 128), :]
    kv_copy.wait()
    ka[0:64, :] = (kvall[0:64, :].astype(F32) * 0.125).astype(BF16)
    va[0:64, :] = kvall[64:128, :]
    kt[...] = jnp.transpose(ka[...].astype(F32)).astype(BF16)

    def attend(quarter, slot):
        def block(j, carry):
            lanes = pl.ds(pl.multiple_of(quarter * QUARTER + j * LB, LB), LB)
            scores = dot(kt[...], qa[:, lanes])
            peak = jnp.max(scores, axis=0, keepdims=True)
            probs = jnp.exp(scores - peak).astype(BF16)
            both = dot(va[...], probs)
            total = both[64:65, :]
            here = pl.ds(pl.multiple_of(j * LB, LB), LB)
            xsend[slot, :, here] = (both[0:64, :] / total).astype(BF16)
            xlse_send[slot, :, here] = peak + jnp.log(total)
            return carry

        lax.fori_loop(0, QUARTER // LB, block, 0)

    def x_copies(i):
        device = at_x(i)
        return (
            pltpu.make_async_remote_copy(
                src_ref=xsend.at[i], dst_ref=xrecv.at[i], send_sem=xs.at[i], recv_sem=xr.at[i],
                device_id=device, device_id_type=MESH),
            pltpu.make_async_remote_copy(
                src_ref=xlse_send.at[i], dst_ref=xlse.at[i], send_sem=xls.at[i], recv_sem=xlr.at[i],
                device_id=device, device_id_type=MESH),
        )

    def peer_quarter(i, carry):
        attend(lax.rem(x + i, NX), i)
        for copy in x_copies(i):
            copy.start()
        return carry

    lax.fori_loop(1, NX, peer_quarter, 0)
    attend(x, 0)

    def merge(parts, lses):
        peak = lses[0]
        for v in lses[1:]:
            peak = jnp.maximum(peak, v)
        total = jnp.zeros_like(peak)
        out = None
        for part, v in zip(parts, lses):
            weight = jnp.exp(v - peak)
            total = total + weight
            term = part.astype(F32) * weight
            out = term if out is None else out + term
        return out / total, peak + jnp.log(total)

    for i in range(1, NX):
        for copy in x_copies(i):
            copy.wait()
    for b in range(4):
        lanes = slice(128 * b, 128 * b + 128)
        out, lse = merge(
            [xsend[0, :, lanes]] + [xrecv[i, :, lanes] for i in range(1, NX)],
            [xlse_send[0, :, lanes]] + [xlse[i, :, lanes] for i in range(1, NX)],
        )
        zsend[:, lanes] = out.astype(BF16)
        zlse_send[b] = lse

    def tile_of(zz):
        a, b = zz // 4, lax.rem(zz, 4)
        return pl.ds(pl.multiple_of(16 * a, 16), 16), pl.ds(pl.multiple_of(128 * b, 128), 128), b

    def z_copies(i):
        rows, lanes, b = tile_of(lax.rem(z + i, NZ))
        device = at_z(i)
        return (
            pltpu.make_async_remote_copy(
                src_ref=zsend.at[rows, lanes], dst_ref=zrecv.at[i], send_sem=zs.at[i],
                recv_sem=zr.at[i], device_id=device, device_id_type=MESH),
            pltpu.make_async_remote_copy(
                src_ref=zlse_send.at[b], dst_ref=zlse.at[i], send_sem=zls.at[i],
                recv_sem=zlr.at[i], device_id=device, device_id_type=MESH),
        )

    def z_start(i, carry):
        for copy in z_copies(i):
            copy.start()
        return carry

    def z_wait(i, carry):
        for copy in z_copies(i):
            copy.wait()
        return carry

    lax.fori_loop(1, NZ, z_start, 0)
    my_rows, my_lanes, my_b = tile_of(z)
    zrecv[0] = zsend[my_rows, my_lanes]
    zlse[0] = zlse_send[my_b]
    lax.fori_loop(1, NZ, z_wait, 0)
    out, _ = merge([zrecv[i] for i in range(NZ)], [zlse[i] for i in range(NZ)])

    def out_tile(zz):
        rows, _, b = tile_of(zz)
        return rows, pl.ds(pl.multiple_of(512 * x + 128 * b, 128), 128)

    rows, lanes = out_tile(z)
    att_ref[rows, lanes] = out.astype(BF16)

    def a_copy(i, zz):
        tile = att_ref.at[out_tile(zz)]
        return pltpu.make_async_remote_copy(
            src_ref=tile, dst_ref=tile, send_sem=as_.at[i], recv_sem=ar.at[i],
            device_id=at_z(i), device_id_type=MESH)

    def spread(zz):
        tile = att_ref.at[out_tile(zz)]
        for i in range(1, NX):
            remote(tile, tile, bs.at[i], br.at[i], at_x(i))

    def a_start(i, carry):
        a_copy(i, z).start()
        return carry

    def a_forward(i, carry):
        zz = lax.rem(z + NZ - i, NZ)
        a_copy(i, zz).wait_recv()
        spread(zz)
        return carry

    def a_done(i, carry):
        a_copy(i, z).wait_send()
        return carry

    lax.fori_loop(1, NZ, a_start, 0)
    spread(z)
    lax.fori_loop(1, NZ, a_forward, 0)
    for i in range(1, NX):
        quarter = att_ref.at[:, pl.ds(pl.multiple_of(512 * x, 512), 512)]
        whole = pltpu.make_async_remote_copy(
            src_ref=quarter, dst_ref=quarter, send_sem=bs.at[i], recv_sem=br.at[i],
            device_id=at_x(i), device_id_type=MESH)
        whole.wait_recv()
        whole.wait_send()
    lax.fori_loop(1, NZ, a_done, 0)
    feature_copy.wait()


def on_device(recording, spatial_w, conv_w, conv_b, dilations, valid_frames, key_w, value_w, queries):
    vmem = pl.BlockSpec(memory_space=pltpu.VMEM)
    smem = pl.BlockSpec(memory_space=pltpu.SMEM)
    dma = pltpu.SemaphoreType.DMA
    V = pltpu.VMEM
    return pl.pallas_call(
        kernel,
        out_shape=(
            jax.ShapeDtypeStruct((64, 1024), BF16),
            jax.ShapeDtypeStruct((64, LATENTS), BF16),
        ),
        in_specs=[smem, smem] + [vmem] * 7,
        out_specs=(vmem, vmem),
        scratch_shapes=[
            V((32, 512), BF16), V((256, 512), BF16), V((512, 256), BF16), V((256, 768), BF16),
            V((3, 3, 128, 512), BF16), V((2, 8, 128), F32), V((256, 512), BF16),
            V((512, 768), BF16), V((512, 640), BF16), V((512, 640), BF16), V((512, 512), BF16),
            V((384, 768), F32), V((128, 768), F32),
            V((256, 512), BF16), V((128, 1024), BF16),
            V((128, 1024), BF16), V((1024, 128), BF16), V((80, 1024), BF16), V((128, LATENTS), BF16),
            V((4, 64, 512), BF16), V((4, 1, 512), F32), V((4, 64, 512), BF16), V((4, 1, 512), F32),
            V((64, 512), BF16), V((4, 1, 128), F32), V((16, 16, 128), BF16), V((16, 1, 128), F32),
            dma((7,)), dma((7,)), dma((15,)), dma((15,)), dma((4,)), dma((4,)), dma((4,)),
            dma((9,)), dma((9,)), dma, dma, dma, dma,
            dma((4,)), dma((4,)), dma((4,)), dma((4,)),
            dma((16,)), dma((16,)), dma((16,)), dma((16,)),
            dma((16,)), dma((16,)), dma((4,)), dma((4,)),
        ],
        compiler_params=pltpu.CompilerParams(
            collective_id=0, has_side_effects=True, vmem_limit_bytes=56 * 2**20
        ),
        name="encoder",
    )(dilations, valid_frames, recording, spatial_w, conv_w, conv_b, key_w, value_w, queries)


def solution(mesh):
    return jax.shard_map(
        on_device,
        mesh=mesh,
        in_specs=(
            P("sensor", "tm"),
            P(None, "sensor"),
            P(None, None, "sensor", None),
            P(None, "sensor"),
            P(),
            P("tm"),
            P("sensor", None),
            P("sensor", None),
            P("sensor", None),
        ),
        out_specs=(P("sensor", "tm"), P("sensor", None)),
        check_vma=False,
    )
```

time: 663 us -> 95.9 us (0.14)
  waiting for transfers between devices: 301 us -> 0 us
  blocking collectives: 283 us -> 0 us
  Pallas kernels: 0 us -> 90.5 us
  matrix products: 25.2 us -> 0 us
  between operations: 20.2 us -> 1.29 us
  starting transfers between devices: 17.7 us -> 0 us
  other arithmetic: 8.78 us -> 0 us
    psum x1 -> x0, blocking collectives: 145 us -> none  [on_device(): lax.psum((totals * rescale, weighted * rescale[:, None, :]), 'tm')]
    pmax x1 -> x0, blocking collectives: 138 us -> none  [on_device(): global_peaks = lax.pmax(peaks, 'tm')]
    psum x1 -> x0, waiting for transfers between devices: 121 us -> none  [on_device(): lax.psum((totals * rescale, weighted * rescale[:, None, :]), 'tm')]
    all_gather x4 -> x0, waiting for transfers between devices: 118 us -> none  [the longest x3 86.8 us: on_device(): lax.all_gather(padded, 'sensor', axis=0, tiled=True)]
    pallas_call x0 -> x1, Pallas kernels: none -> 90.5 us  [on_device(): pl.pallas_call(kernel, out_shape=(jax.ShapeDtypeStruct((64, 1024), BF16),...]
    reduce_scatter x1 -> x0, waiting for transfers between devices: 45.9 us -> none  [on_device(): lax.psum_scatter(jnp.dot(spatial_w, recording, preferred_element_type=jnp...]
    dot_general x20 -> x0, matrix products: 25.2 us -> none  [the longest x9 14.8 us: add_taps(): jnp.dot(kernel, shifted, preferred_element_type=jnp.float32)]
    ppermute x6 -> x0, starting transfers between devices: 17.5 us -> none  [the longest x3 10.4 us: padded_2(): lax.ppermute(tail, axis, [(i, (i + 1) % count) for i in range(ends)])]
  transfers between devices with their start and end apart: 12 -> 0, of which waited for: 9 -> 0; matrix products, arithmetic and copies ran while one was open for 0% -> 0% of each run, Pallas kernels for 0% -> 0%
where the time goes in v1:
time: 95.9 us; the launch traced here: 95.6 us
  Pallas kernels  90.5 us (94%)
  local copies, waits for them, and re-layouts  3.83 us (4%)
  between operations  1.29 us (1%)
    pallas_call x1, Pallas kernels, on_device(): pl.pallas_call(kernel, out_shape=(jax.ShapeDtypeStruct((64, 1024), BF16),...  90.5 us
    unnamed x5, local copies, waits for them, and re-layouts  3.83 us

profile of v1, /device:TPU:6, one launch (start us, length us, event | category | flops | bytes accessed | tf_op | source)
XLA Modules:
  0.0 95.6 jit_solution(8630204382032308092)
XLA Ops:
  1.3 1.5 %copy.11.sw_ref = bf16[512,32]{1,0:T(8,128)(2,1)} copy(bf16[512,32]{0,1:T(8,128)(2,1)} %param.10) | data formatting | bytes 65536 | tf_op args[1]
  2.8 90.5 %encoder.1 = (bf16[64,1024]{1,0:T(8,128)(2,1)}, bf16[64,2048]{1,0:T(8,128)(2,1)}) custom-call(s32[3]{0:T(128)} %dil_ref.1, s32[1]{0:T(128)S(6)} %copy.14.valid_ref, bf16[32,1024]{1,0:T(8,128)(2,1)} %rec_ref.1, bf16[512,32]{1,0:T(8,128)(2,1)} %copy.11.sw_ref, bf16[3,3,64,512]{3,2,1,0:T(8,128)(2,1)} %cw_ref.1, f32[3,64]{1,0:T(4,128)} %cb_ref.1, ...), custom_call_target="tpu_custom_call" | custom-call | tf_op jit(solution)/shard_map/encoder/pallas_call | solution.py:377
  93.3 0.0 copy-start
  93.3 1.6 %copy.15 = bf16[64,1024]{1,0:T(8,128)(2,1)} copy(bf16[64,1024]{1,0:T(8,128)(2,1)} %get-tuple-element.4) | data formatting | bytes 262144
  94.9 0.0 copy-done
  94.9 0.7 copy.16
Async XLA Ops:
  93.3 1.6 %copy-start = (bf16[64,2048]{1,0:T(8,128)(2,1)S(1)}, bf16[64,2048]{1,0:T(8,128)(2,1)}, u32[]{:S(2)}) copy-start(bf16[64,2048]{1,0:T(8,128)(2,1)} %get-tuple-element.5) | copy-start | bytes 786436

commit v2 on v1

v2 whole, which is shorter than its diff:
```python
import jax
import jax.numpy as jnp
from jax import lax
from jax.experimental import pallas as pl
from jax.experimental.pallas import tpu as pltpu
from jax.sharding import PartitionSpec as P

MESH = pl.DeviceIdType.MESH
BF16 = jnp.bfloat16
F32 = jnp.float32
NY, NX, NZ = 4, 4, 16
HD = 64
LATENTS = 2048
QUARTER = 512
LB = 256


def dot(a, b):
    return jnp.dot(a, b, preferred_element_type=F32)


def kernel(
    dil_ref, valid_ref, rec_ref, sw_ref, cw_ref, cb_ref, kw_ref, vw_ref, q_ref,
    feat_ref, att_ref,
    st, sfull, rec, rwin, wc, bias, kvw, h0, h1, h2, h3, taps, kv, kvall, ka, kt, va, qa,
    xsend, xlse_send, xrecv, xlse, zsend, zlse_send, zrecv, zlse,
    loc, rec_s, rec_r, hal_s, hal_r, b_s, b_r, st_s, st_r, sf_s, sf_r, so_s, so_r,
    y_s, y_r, xp_s, xp_r, xm_s, xm_r, o_s, o_r, fy_s, fy_r, fx_s, fx_r,
    f_s, f_r, kv_s, kv_r, z1, z2, z4,
    xs, xr, xls, xlr, zs, zr, zls, zlr, as_, ar, bs, br,
):
    s = lax.axis_index("sensor")
    t = lax.axis_index("tm")
    y, c = s // 2, lax.rem(s, 2)
    z, x = t // NX, lax.rem(t, NX)
    other = 1 - c
    parity = lax.rem(x, 2)

    def at_y(i, core):
        return (lax.rem(y + i, NY) * 2 + core, t)

    def at_x(i):
        return (s, z * NX + lax.rem(x + i, NX))

    def at_z(i):
        return (s, lax.rem(z + i, NZ) * NX + x)

    sibling = (y * 2 + other, t)
    prev_tm = lax.rem(t + 63, 64)
    next_tm = lax.rem(t + 1, 64)
    peers = [(i, k) for i in range(1, NY) for k in range(2)] + [(0, 1)]

    def signal(sem, device):
        pl.semaphore_signal(sem, inc=1, device_id=device, device_id_type=MESH)

    barrier = pltpu.get_barrier_semaphore()
    for i, k in peers:
        signal(barrier, at_y(i, lax.rem(c + k, 2)))
    for i in range(1, NX):
        signal(barrier, at_x(i))
    signal(barrier, at_z(1))
    signal(barrier, at_z(NZ - 1))

    @pl.when((s == 0) | (s == 7))
    def _():
        block = jnp.where(s == 0, prev_tm, next_tm)
        for k in range(8):
            signal(barrier, (k, block))

    def rows(start, size, align):
        return pl.ds(pl.multiple_of(start, align), size)

    def of_head(index):
        return rows(128 * index, 128, 128)

    own_rec = rows(32 * s, 32, 32)
    own_out = rows(64 * s, 64, 64)
    local = [
        pltpu.make_async_copy(cw_ref, wc.at[:, :, own_out, :], loc.at[0]),
        pltpu.make_async_copy(kw_ref, kvw.at[rows(128 * s, 64, 64)], loc.at[1]),
        pltpu.make_async_copy(vw_ref, kvw.at[rows(128 * s + 64, 64, 64)], loc.at[2]),
        pltpu.make_async_copy(q_ref, qa.at[0:64], loc.at[3]),
    ]
    for copy in local:
        copy.start()
    st[own_rec, :] = sw_ref[...]
    bias[s] = jnp.zeros((8, 128), F32)
    bias[s, 0:3, 0:64] = cb_ref[...]

    def rec_window(index):
        start = jnp.clip(index - 1, 0, 5)
        return rows(128 * start, 384, 128), rows(128 * (start - index + 2), 384, 128)

    here_src, here_dst = rec_window(s)
    rec[own_rec, here_dst] = rec_ref[:, here_src]

    pl.semaphore_wait(barrier, 7 + 3 + 2 + 2)

    def remote(src, dst, ssem, rsem, device):
        return pltpu.make_async_remote_copy(
            src_ref=src, dst_ref=dst, send_sem=ssem, recv_sem=rsem,
            device_id=device, device_id_type=MESH,
        )

    def same(ref, ssem, rsem, device):
        return remote(ref, ref, ssem, rsem, device)

    signal(z1.at[0], at_z(1))
    signal(z1.at[1], at_z(NZ - 1))

    def of_sensor(i):
        return lax.rem(y + NY - i, NY) * 2 + c

    st_y = [same(st.at[own_rec], st_s.at[i], st_r.at[i], at_y(i, c)) for i in range(1, NY)]
    st_own = same(st.at[own_rec], so_s, so_r, sibling)
    for copy in st_y:
        copy.start()
    st_own.start()
    rec_copies = []
    for n, (i, k) in enumerate(peers):
        core = lax.rem(c + k, 2)
        src, dst = rec_window(lax.rem(y + i, NY) * 2 + core)
        rec_copies.append(
            remote(rec_ref.at[:, src], rec.at[own_rec, dst], rec_s.at[n], rec_r.at[n], at_y(i, core))
        )
    halo = [
        remote(rec_ref.at[:, 896:1024], rec.at[own_rec, 128:256], hal_s.at[0], hal_r.at[s], (0, next_tm)),
        remote(rec_ref.at[:, 0:128], rec.at[own_rec, 384:512], hal_s.at[1], hal_r.at[s], (7, prev_tm)),
    ]
    bias_copies = [
        same(bias.at[s], b_s.at[n], b_r.at[n], at_y(i, lax.rem(c + k, 2)))
        for n, (i, k) in enumerate(peers)
    ]
    for copy in halo + rec_copies + bias_copies:
        copy.start()
    for copy in local:
        copy.wait()

    def piece(g, index, start, count):
        if g < 3:
            return wc.at[g, :, rows(64 * index + 16 * start, 16 * count, 16), :]
        return kvw.at[rows(128 * index + 32 * start, 32 * count, 32), :]

    def y_copies(g):
        return [
            same(piece(g, s, 2 * parity, 2), y_s.at[g, i], y_r.at[g, i], at_y(i, c))
            for i in range(1, NY)
        ]

    def own_copy(g):
        return same(piece(g, s, 0, 4), o_s.at[g], o_r.at[g], sibling)

    def issue(g):
        for copy in y_copies(g):
            copy.start()
        own_copy(g).start()

    def x_plus(g, i):
        return same(piece(g, of_sensor(i), 2 * parity, 1), xp_s.at[g, i], xp_r.at[g, i], at_x(1))

    def x_minus(g, i):
        return same(piece(g, of_sensor(i), 2 * parity + 1, 1), xm_s.at[g, i], xm_r.at[g, i], at_x(3))

    def sib_y(g, i):
        return same(piece(g, of_sensor(i), 2 * parity, 2), fy_s.at[g, i], fy_r.at[g, i], sibling)

    def sib_x(g, i):
        return same(piece(g, of_sensor(i), 2 - 2 * parity, 2), fx_s.at[g, i], fx_r.at[g, i], sibling)

    def forward_y(g):
        copies = y_copies(g)
        for i in (1, 3, 2):
            copies[i - 1].wait_recv()
            x_plus(g, i).start()
            x_minus(g, i).start()
            sib_y(g, i).start()

    def forward_x(g):
        for i in (1, 3, 2):
            x_plus(g, i).wait_recv()
            x_minus(g, i).wait_recv()
            sib_x(g, i).start()

    def ready(g):
        own_copy(g).wait_recv()
        for i in range(1, NY):
            sib_y(g, i).wait_recv()
            sib_x(g, i).wait_recv()

    def sent(g):
        for copy in y_copies(g):
            copy.wait_send()
        own_copy(g).wait_send()
        for i in range(1, NY):
            for copy in (x_plus, x_minus, sib_y, sib_x):
                copy(g, i).wait_send()

    issue(0)
    issue(1)

    first = lax.broadcasted_iota(jnp.int32, (64, LATENTS), 0) == 0
    qa[64:128, :] = jnp.where(first, 1.0, 0.0).astype(BF16)
    va[64:80, :] = jnp.ones((16, 1024), BF16)
    frame = lax.broadcasted_iota(jnp.int32, (64, 1024), 1)
    row = lax.broadcasted_iota(jnp.int32, (64, 1024), 0)
    ka[64:128, :] = jnp.where((row == 0) & (frame >= valid_ref[0]), -1e30, 0.0).astype(BF16)

    def sib_st(i):
        return same(
            st.at[rows(32 * of_sensor(i), 32, 32)], sf_s.at[i], sf_r.at[i], sibling
        )

    for i in (1, 3, 2):
        st_y[i - 1].wait_recv()
        sib_st(i).start()
    for copy in rec_copies:
        copy.wait_recv()

    @pl.when((s == 0) | (s == 7))
    def _():
        for k in range(8):
            tile = rec.at[0:32, 0:128]
            pltpu.make_async_copy(tile, tile, hal_r.at[k]).wait()

    def turned(tiles, count, amount):
        lane = lax.broadcasted_iota(jnp.int32, tiles[0].shape, 1)
        keep = lane < 128 - amount
        turn = lax.rem(128 - amount, 128)
        rolled = [pltpu.roll(tile, turn, 1) for tile in tiles]
        last = len(tiles) - 1
        return [jnp.where(keep, rolled[k], rolled[min(k + 1, last)]) for k in range(count)]

    window = turned(
        [rec[:, 128 * k : 128 * k + 128].astype(F32) for k in range(1, 4)], 2, jnp.int32(64)
    )
    for k in range(2):
        rwin[:, 128 * k : 128 * k + 128] = window[k].astype(BF16)

    low = jnp.where((t == 0) & (s == 0), 0, -4096)
    high = jnp.where((t == 63) & (s == 7), 128, 4096)

    def inside(lanes, start):
        f = lax.broadcasted_iota(jnp.int32, (128, lanes), 1) + start
        return (f >= low) & (f < high)

    st_own.wait_recv()
    for i in range(1, NY):
        sib_st(i).wait_recv()
    sfull[...] = jnp.transpose(st[...].astype(F32)).astype(BF16)
    for n in range(0, 512, 128):
        part = dot(sfull[n : n + 128, :], rwin[...])
        h0[n : n + 128, :] = jnp.where(inside(256, -64), part, 0.0).astype(BF16)

    for copy in bias_copies:
        copy.wait_recv()
    all_bias = jnp.transpose(
        jnp.concatenate([bias[k][:, 0:64] for k in range(8)], axis=1)
    )

    def conv(layer, source, target, offset, tiles, start):
        d = dil_ref[layer]
        for n in range(0, 512, 128):
            w = wc[layer, :, n : n + 128, :].reshape(384, 512)
            taps[...] = dot(w, source[...])
            a, b, e = [
                turned(
                    [taps[128 * j : 128 * j + 128, 128 * k : 128 * k + 128] for k in range(2)],
                    tiles, offset + (j - 1) * d,
                )
                for j in range(3)
            ]
            r = turned(
                [source[n : n + 128, 128 * k : 128 * k + 128].astype(F32) for k in range(2)],
                tiles, jnp.int32(offset),
            )
            col = all_bias[n : n + 128, layer : layer + 1]
            for k in range(tiles):
                pre = col + a[k] + b[k] + e[k]
                out = r[k] + 0.5 * pre * (1.0 + lax.erf(pre * 0.7071067811865476))
                out = jnp.where(inside(128, start + 128 * k), out, 0.0)
                target[n : n + 128, 128 * k : 128 * k + 128] = out.astype(BF16)

    forward_y(0)
    issue(2)
    pl.semaphore_wait(z1.at[0], 1)
    pl.semaphore_wait(z1.at[1], 1)
    signal(z2.at[0], at_z(2))
    signal(z2.at[1], at_z(NZ - 2))
    forward_y(1)
    issue(3)
    forward_x(0)
    ready(0)
    conv(0, h0, h1, 16, 2, -48)
    forward_y(2)
    forward_x(1)
    pl.semaphore_wait(z2.at[0], 1)
    pl.semaphore_wait(z2.at[1], 1)
    signal(z4.at[0], at_z(4))
    signal(z4.at[1], at_z(NZ - 4))
    ready(1)
    conv(1, h1, h2, 16, 2, -32)
    forward_y(3)
    forward_x(2)
    ready(2)
    conv(2, h2, h3, 32, 1, 0)
    forward_x(3)
    ready(3)

    own_lanes = rows(128 * s, 128, 128)
    for n in range(0, 1024, 256):
        kv[n : n + 256, :] = dot(kvw[n : n + 256, :], h3[...]).astype(BF16)
    kv_copies = []
    feature_copies = []
    for n, (i, k) in enumerate(peers):
        core = lax.rem(c + k, 2)
        to = lax.rem(y + i, NY) * 2 + core
        kv_copies.append(
            remote(kv.at[of_head(to)], kvall.at[:, own_lanes], kv_s.at[n], kv_r.at[n], at_y(i, core))
        )
        feature_copies.append(
            remote(
                h3.at[rows(64 * to, 64, 64)], feat_ref.at[:, own_lanes],
                f_s.at[n], f_r.at[n], at_y(i, core),
            )
        )
    for copy in kv_copies + feature_copies:
        copy.start()
    kvall[:, own_lanes] = kv[of_head(s), :]
    feat_ref[:, own_lanes] = h3[own_out, :]
    pl.semaphore_wait(z4.at[0], 1)
    pl.semaphore_wait(z4.at[1], 1)
    for copy in st_y + [st_own] + rec_copies + halo + bias_copies:
        copy.wait_send()
    for i in range(1, NY):
        sib_st(i).wait_send()
    for g in range(4):
        sent(g)
    for copy in kv_copies:
        copy.wait()
    ka[0:64, :] = (kvall[0:64, :].astype(F32) * 0.125).astype(BF16)
    va[0:64, :] = kvall[64:128, :]
    kt[...] = jnp.transpose(ka[...].astype(F32)).astype(BF16)

    def attend(quarter, slot):
        def block(j, carry):
            lanes = pl.ds(pl.multiple_of(quarter * QUARTER + j * LB, LB), LB)
            scores = dot(kt[...], qa[:, lanes])
            peak = jnp.max(scores, axis=0, keepdims=True)
            probs = jnp.exp(scores - peak).astype(BF16)
            both = dot(va[...], probs)
            total = both[64:65, :]
            here = pl.ds(pl.multiple_of(j * LB, LB), LB)
            xsend[slot, :, here] = (both[0:64, :] / total).astype(BF16)
            xlse_send[slot, :, here] = peak + jnp.log(total)
            return carry

        lax.fori_loop(0, QUARTER // LB, block, 0)

    def x_copies(i):
        device = at_x(i)
        return (
            pltpu.make_async_remote_copy(
                src_ref=xsend.at[i], dst_ref=xrecv.at[i], send_sem=xs.at[i], recv_sem=xr.at[i],
                device_id=device, device_id_type=MESH),
            pltpu.make_async_remote_copy(
                src_ref=xlse_send.at[i], dst_ref=xlse.at[i], send_sem=xls.at[i], recv_sem=xlr.at[i],
                device_id=device, device_id_type=MESH),
        )

    def peer_quarter(i, carry):
        attend(lax.rem(x + i, NX), i)
        for copy in x_copies(i):
            copy.start()
        return carry

    lax.fori_loop(1, NX, peer_quarter, 0)
    attend(x, 0)

    def merge(parts, lses):
        peak = lses[0]
        for v in lses[1:]:
            peak = jnp.maximum(peak, v)
        total = jnp.zeros_like(peak)
        out = None
        for part, v in zip(parts, lses):
            weight = jnp.exp(v - peak)
            total = total + weight
            term = part.astype(F32) * weight
            out = term if out is None else out + term
        return out / total, peak + jnp.log(total)

    for i in range(1, NX):
        for copy in x_copies(i):
            copy.wait()
    for b in range(4):
        lanes = slice(128 * b, 128 * b + 128)
        out, lse = merge(
            [xsend[0, :, lanes]] + [xrecv[i, :, lanes] for i in range(1, NX)],
            [xlse_send[0, :, lanes]] + [xlse[i, :, lanes] for i in range(1, NX)],
        )
        zsend[:, lanes] = out.astype(BF16)
        zlse_send[b] = lse

    def tile_of(zz):
        a, b = zz // 4, lax.rem(zz, 4)
        return pl.ds(pl.multiple_of(16 * a, 16), 16), pl.ds(pl.multiple_of(128 * b, 128), 128), b

    def z_copies(i):
        rows, lanes, b = tile_of(lax.rem(z + i, NZ))
        device = at_z(i)
        return (
            pltpu.make_async_remote_copy(
                src_ref=zsend.at[rows, lanes], dst_ref=zrecv.at[i], send_sem=zs.at[i],
                recv_sem=zr.at[i], device_id=device, device_id_type=MESH),
            pltpu.make_async_remote_copy(
                src_ref=zlse_send.at[b], dst_ref=zlse.at[i], send_sem=zls.at[i],
                recv_sem=zlr.at[i], device_id=device, device_id_type=MESH),
        )

    def far_first(n):
        k = (n + 1) // 2
        return 8 + k * (1 - 2 * lax.rem(n, 2))

    def near_first(n):
        return far_first(14 - n)

    def z_start(n, carry):
        for copy in z_copies(far_first(n)):
            copy.start()
        return carry

    def z_wait(n, carry):
        for copy in z_copies(near_first(n)):
            copy.wait()
        return carry

    lax.fori_loop(0, NZ - 1, z_start, 0)
    my_rows, my_lanes, my_b = tile_of(z)
    zrecv[0] = zsend[my_rows, my_lanes]
    zlse[0] = zlse_send[my_b]
    lax.fori_loop(0, NZ - 1, z_wait, 0)
    out, _ = merge([zrecv[i] for i in range(NZ)], [zlse[i] for i in range(NZ)])

    def out_tile(zz):
        rows, _, b = tile_of(zz)
        return rows, pl.ds(pl.multiple_of(512 * x + 128 * b, 128), 128)

    rows, lanes = out_tile(z)
    att_ref[rows, lanes] = out.astype(BF16)

    def a_copy(i, zz):
        tile = att_ref.at[out_tile(zz)]
        return pltpu.make_async_remote_copy(
            src_ref=tile, dst_ref=tile, send_sem=as_.at[i], recv_sem=ar.at[i],
            device_id=at_z(i), device_id_type=MESH)

    def spread(zz):
        tile = att_ref.at[out_tile(zz)]
        for i in range(1, NX):
            remote(tile, tile, bs.at[i], br.at[i], at_x(i)).start()

    def a_start(n, carry):
        a_copy(far_first(n), z).start()
        return carry

    def a_forward(n, carry):
        i = near_first(n)
        zz = lax.rem(z + NZ - i, NZ)
        a_copy(i, zz).wait_recv()
        spread(zz)
        return carry

    def a_done(i, carry):
        a_copy(i, z).wait_send()
        return carry

    lax.fori_loop(0, NZ - 1, a_start, 0)
    spread(z)
    lax.fori_loop(0, NZ - 1, a_forward, 0)
    for i in range(1, NX):
        quarter = att_ref.at[:, pl.ds(pl.multiple_of(512 * x, 512), 512)]
        whole = pltpu.make_async_remote_copy(
            src_ref=quarter, dst_ref=quarter, send_sem=bs.at[i], recv_sem=br.at[i],
            device_id=at_x(i), device_id_type=MESH)
        whole.wait_recv()
        whole.wait_send()
    lax.fori_loop(1, NZ, a_done, 0)
    for copy in feature_copies:
        copy.wait()


def on_device(recording, spatial_w, conv_w, conv_b, dilations, valid_frames, key_w, value_w, queries):
    vmem = pl.BlockSpec(memory_space=pltpu.VMEM)
    smem = pl.BlockSpec(memory_space=pltpu.SMEM)
    hbm = pl.BlockSpec(memory_space=pl.ANY)
    dma = pltpu.SemaphoreType.DMA
    regular = pltpu.SemaphoreType.REGULAR
    V = pltpu.VMEM
    return pl.pallas_call(
        kernel,
        out_shape=(
            jax.ShapeDtypeStruct((64, 1024), BF16),
            jax.ShapeDtypeStruct((64, LATENTS), BF16),
        ),
        in_specs=[smem, smem, vmem, vmem, hbm, vmem, hbm, hbm, hbm],
        out_specs=(vmem, vmem),
        scratch_shapes=[
            V((256, 512), BF16), V((512, 256), BF16), V((256, 640), BF16), V((256, 256), BF16),
            V((3, 3, 512, 512), BF16), V((8, 8, 128), F32), V((1024, 512), BF16),
            V((512, 256), BF16), V((512, 256), BF16), V((512, 256), BF16), V((512, 128), BF16),
            V((384, 256), F32), V((1024, 128), BF16), V((128, 1024), BF16),
            V((128, 1024), BF16), V((1024, 128), BF16), V((80, 1024), BF16), V((128, LATENTS), BF16),
            V((4, 64, 512), BF16), V((4, 1, 512), F32), V((4, 64, 512), BF16), V((4, 1, 512), F32),
            V((64, 512), BF16), V((4, 1, 128), F32), V((16, 16, 128), BF16), V((16, 1, 128), F32),
            dma((4,)), dma((7,)), dma((7,)), dma((2,)), dma((8,)), dma((7,)), dma((7,)),
            dma((4,)), dma((4,)), dma((4,)), dma((4,)), dma, dma,
            dma((4, 4)), dma((4, 4)), dma((4, 4)), dma((4, 4)), dma((4, 4)), dma((4, 4)),
            dma((4,)), dma((4,)), dma((4, 4)), dma((4, 4)), dma((4, 4)), dma((4, 4)),
            dma((7,)), dma((7,)), dma((7,)), dma((7,)),
            regular((2,)), regular((2,)), regular((2,)),
            dma((4,)), dma((4,)), dma((4,)), dma((4,)),
            dma((16,)), dma((16,)), dma((16,)), dma((16,)),
            dma((16,)), dma((16,)), dma((4,)), dma((4,)),
        ],
        compiler_params=pltpu.CompilerParams(
            collective_id=0, has_side_effects=True, vmem_limit_bytes=56 * 2**20
        ),
        name="encoder",
    )(dilations, valid_frames, recording, spatial_w.T, conv_w, conv_b, key_w, value_w, queries)


def solution(mesh):
    return jax.shard_map(
        on_device,
        mesh=mesh,
        in_specs=(
            P("sensor", "tm"),
            P(None, "sensor"),
            P(None, None, "sensor", None),
            P(None, "sensor"),
            P(),
            P("tm"),
            P("sensor", None),
            P("sensor", None),
            P("sensor", None),
        ),
        out_specs=(P("sensor", "tm"), P("sensor", None)),
        check_vma=False,
    )
```

time: 95.9 us -> 82.4 us (0.86); the launches traced: 95.6 us -> 81.1 us
  Pallas kernels: 90.5 us -> 77.5 us
  local copies, waits for them, and re-layouts: 3.83 us -> 2.32 us
    pallas_call x1, Pallas kernels: 90.5 us -> 77.5 us  [on_device(): pl.pallas_call(kernel, out_shape=(jax.ShapeDtypeStruct((64, 1024), BF16),...]
    unnamed x5 -> x4, local copies, waits for them, and re-layouts: 3.83 us -> 2.32 us
where the time goes in v2:
time: 82.4 us; the launch traced here: 81.1 us
  Pallas kernels  77.5 us (94%)
  local copies, waits for them, and re-layouts  2.32 us (3%)
  between operations  1.29 us (2%)
    pallas_call x1, Pallas kernels, on_device(): pl.pallas_call(kernel, out_shape=(jax.ShapeDtypeStruct((64, 1024), BF16),...  77.5 us
    unnamed x4, local copies, waits for them, and re-layouts  2.32 us

profile of v2, /device:TPU:6, one launch (start us, length us, event | category | flops | bytes accessed | tf_op | source)
XLA Modules:
  0.0 81.1 jit_solution(15271112268684845083)
XLA Ops:
  1.3 77.5 %encoder.1 = (bf16[64,1024]{1,0:T(8,128)(2,1)}, bf16[64,2048]{1,0:T(8,128)(2,1)}) custom-call(s32[3]{0:T(128)} %dil_ref.1, s32[1]{0:T(128)S(6)} %copy.13.valid_ref, bf16[32,1024]{1,0:T(8,128)(2,1)} %rec_ref.1, bf16[32,512]{1,0:T(8,128)(2,1)} %bitcast.1, bf16[3,3,64,512]{3,2,1,0:T(8,128)(2,1)} %cw_ref.1, f32[3,64]{1,0:T(4,128)} %cb_ref.1, ...), custom_call_target="tpu_custom_call" | custom-call | tf_op jit(solution)/shard_map/encoder/pallas_call | solution.py:499
  78.8 0.0 copy-start
  78.8 1.6 %copy.14 = bf16[64,1024]{1,0:T(8,128)(2,1)} copy(bf16[64,1024]{1,0:T(8,128)(2,1)} %get-tuple-element.4) | data formatting | bytes 262144
  80.4 0.0 copy-done
  80.4 0.7 copy.15
Async XLA Ops:
  78.8 1.6 %copy-start = (bf16[64,2048]{1,0:T(8,128)(2,1)S(1)}, bf16[64,2048]{1,0:T(8,128)(2,1)}, u32[]{:S(2)}) copy-start(bf16[64,2048]{1,0:T(8,128)(2,1)} %get-tuple-element.5) | copy-start | bytes 786436

commit v3 on v2

--- a/solution.py
+++ b/solution.py
@@ -25,7 +25,7 @@
     st, sfull, rec, rwin, wc, bias, kvw, h0, h1, h2, h3, taps, kv, kvall, ka, kt, va, qa,
     xsend, xlse_send, xrecv, xlse, zsend, zlse_send, zrecv, zlse,
     loc, rec_s, rec_r, hal_s, hal_r, b_s, b_r, st_s, st_r, sf_s, sf_r, so_s, so_r,
-    y_s, y_r, xp_s, xp_r, xm_s, xm_r, o_s, o_r, fy_s, fy_r, fx_s, fx_r,
+    y_s, y_r, o_s, o_r, r_s, r_r, c_s, c_r,
     f_s, f_r, kv_s, kv_r, z1, z2, z4,
     xs, xr, xls, xlr, zs, zr, zls, zlr, as_, ar, bs, br,
 ):
@@ -113,9 +113,6 @@
 
     st_y = [same(st.at[own_rec], st_s.at[i], st_r.at[i], at_y(i, c)) for i in range(1, NY)]
     st_own = same(st.at[own_rec], so_s, so_r, sibling)
-    for copy in st_y:
-        copy.start()
-    st_own.start()
     rec_copies = []
     for n, (i, k) in enumerate(peers):
         core = lax.rem(c + k, 2)
@@ -131,19 +128,21 @@
         same(bias.at[s], b_s.at[n], b_r.at[n], at_y(i, lax.rem(c + k, 2)))
         for n, (i, k) in enumerate(peers)
     ]
-    for copy in halo + rec_copies + bias_copies:
-        copy.start()
-    for copy in local:
-        copy.wait()
-
-    def piece(g, index, start, count):
+    def colour(g):
+        return lax.rem(x + 2 * z, 4) if g % 2 == 0 else lax.rem(2 * x + z, 4)
+
+    def along(g):
+        ways = ((at_x(1), at_x(NX - 1)), (at_z(1), at_z(NZ - 1)))
+        return ways if g % 2 == 0 else ways[::-1]
+
+    def piece(g, index, quarter, count=1, lanes=slice(0, 512)):
         if g < 3:
-            return wc.at[g, :, rows(64 * index + 16 * start, 16 * count, 16), :]
-        return kvw.at[rows(128 * index + 32 * start, 32 * count, 32), :]
+            return wc.at[g, :, rows(64 * index + 16 * quarter, 16 * count, 16), lanes]
+        return kvw.at[rows(128 * index + 32 * quarter, 32 * count, 32), lanes]
 
     def y_copies(g):
         return [
-            same(piece(g, s, 2 * parity, 2), y_s.at[g, i], y_r.at[g, i], at_y(i, c))
+            same(piece(g, s, colour(g)), y_s.at[g, i], y_r.at[g, i], at_y(i, c))
             for i in range(1, NY)
         ]
 
@@ -155,48 +154,63 @@
             copy.start()
         own_copy(g).start()
 
-    def x_plus(g, i):
-        return same(piece(g, of_sensor(i), 2 * parity, 1), xp_s.at[g, i], xp_r.at[g, i], at_x(1))
-
-    def x_minus(g, i):
-        return same(piece(g, of_sensor(i), 2 * parity + 1, 1), xm_s.at[g, i], xm_r.at[g, i], at_x(3))
-
-    def sib_y(g, i):
-        return same(piece(g, of_sensor(i), 2 * parity, 2), fy_s.at[g, i], fy_r.at[g, i], sibling)
-
-    def sib_x(g, i):
-        return same(piece(g, of_sensor(i), 2 - 2 * parity, 2), fx_s.at[g, i], fx_r.at[g, i], sibling)
+    def relays(g, i):
+        (next_full, prev_full), (next_half, prev_half) = along(g)
+        full = piece(g, of_sensor(i), colour(g))
+        low_half = piece(g, of_sensor(i), colour(g), 1, slice(0, 256))
+        high_half = piece(g, of_sensor(i), colour(g), 1, slice(256, 512))
+        return [
+            same(full, r_s.at[g, i, 0], r_r.at[g, i, 0], next_full),
+            same(full, r_s.at[g, i, 1], r_r.at[g, i, 1], prev_full),
+            same(low_half, r_s.at[g, i, 2], r_r.at[g, i, 2], next_half),
+            same(high_half, r_s.at[g, i, 3], r_r.at[g, i, 3], prev_half),
+        ]
+
+    def to_sibling(g, i, k):
+        quarter = lax.rem(colour(g) + k, 4)
+        return same(piece(g, of_sensor(i), quarter), c_s.at[g, i, k], c_r.at[g, i, k], sibling)
 
     def forward_y(g):
         copies = y_copies(g)
         for i in (1, 3, 2):
             copies[i - 1].wait_recv()
-            x_plus(g, i).start()
-            x_minus(g, i).start()
-            sib_y(g, i).start()
-
-    def forward_x(g):
+            for copy in relays(g, i):
+                copy.start()
+            to_sibling(g, i, 0).start()
+
+    def forward_relays(g):
         for i in (1, 3, 2):
-            x_plus(g, i).wait_recv()
-            x_minus(g, i).wait_recv()
-            sib_x(g, i).start()
+            copies = relays(g, i)
+            copies[0].wait_recv()
+            to_sibling(g, i, 3).start()
+            copies[1].wait_recv()
+            to_sibling(g, i, 1).start()
+            copies[2].wait_recv()
+            copies[3].wait_recv()
+            to_sibling(g, i, 2).start()
 
     def ready(g):
         own_copy(g).wait_recv()
         for i in range(1, NY):
-            sib_y(g, i).wait_recv()
-            sib_x(g, i).wait_recv()
+            for k in range(4):
+                to_sibling(g, i, k).wait_recv()
 
     def sent(g):
         for copy in y_copies(g):
             copy.wait_send()
         own_copy(g).wait_send()
         for i in range(1, NY):
-            for copy in (x_plus, x_minus, sib_y, sib_x):
-                copy(g, i).wait_send()
-
+            for copy in relays(g, i):
+                copy.wait_send()
+            for k in range(4):
+                to_sibling(g, i, k).wait_send()
+
+
+    for copy in local:
+        copy.wait()
     issue(0)
-    issue(1)
+    for copy in st_y + [st_own] + halo + rec_copies + bias_copies:
+        copy.start()
 
     first = lax.broadcasted_iota(jnp.int32, (64, LATENTS), 0) == 0
     qa[64:128, :] = jnp.where(first, 1.0, 0.0).astype(BF16)
@@ -210,6 +224,8 @@
             st.at[rows(32 * of_sensor(i), 32, 32)], sf_s.at[i], sf_r.at[i], sibling
         )
 
+    forward_y(0)
+    issue(1)
     for i in (1, 3, 2):
         st_y[i - 1].wait_recv()
         sib_st(i).start()
@@ -280,19 +296,18 @@
                 out = jnp.where(inside(128, start + 128 * k), out, 0.0)
                 target[n : n + 128, 128 * k : 128 * k + 128] = out.astype(BF16)
 
-    forward_y(0)
+    forward_y(1)
     issue(2)
     pl.semaphore_wait(z1.at[0], 1)
     pl.semaphore_wait(z1.at[1], 1)
     signal(z2.at[0], at_z(2))
     signal(z2.at[1], at_z(NZ - 2))
-    forward_y(1)
-    issue(3)
-    forward_x(0)
+    forward_relays(0)
     ready(0)
     conv(0, h0, h1, 16, 2, -48)
     forward_y(2)
-    forward_x(1)
+    issue(3)
+    forward_relays(1)
     pl.semaphore_wait(z2.at[0], 1)
     pl.semaphore_wait(z2.at[1], 1)
     signal(z4.at[0], at_z(4))
@@ -300,10 +315,10 @@
     ready(1)
     conv(1, h1, h2, 16, 2, -32)
     forward_y(3)
-    forward_x(2)
+    forward_relays(2)
     ready(2)
     conv(2, h2, h3, 32, 1, 0)
-    forward_x(3)
+    forward_relays(3)
     ready(3)
 
     own_lanes = rows(128 * s, 128, 128)
@@ -514,8 +529,8 @@
             V((64, 512), BF16), V((4, 1, 128), F32), V((16, 16, 128), BF16), V((16, 1, 128), F32),
             dma((4,)), dma((7,)), dma((7,)), dma((2,)), dma((8,)), dma((7,)), dma((7,)),
             dma((4,)), dma((4,)), dma((4,)), dma((4,)), dma, dma,
-            dma((4, 4)), dma((4, 4)), dma((4, 4)), dma((4, 4)), dma((4, 4)), dma((4, 4)),
-            dma((4,)), dma((4,)), dma((4, 4)), dma((4, 4)), dma((4, 4)), dma((4, 4)),
+            dma((4, 4)), dma((4, 4)), dma((4,)), dma((4,)),
+            dma((4, 4, 4)), dma((4, 4, 4)), dma((4, 4, 4)), dma((4, 4, 4)),
             dma((7,)), dma((7,)), dma((7,)), dma((7,)),
             regular((2,)), regular((2,)), regular((2,)),
             dma((4,)), dma((4,)), dma((4,)), dma((4,)),

time: 82.4 us -> 79.7 us (0.967)
  Pallas kernels: 77.5 us -> 74.6 us
    pallas_call x1, Pallas kernels: 77.5 us -> 74.6 us  [on_device(): pl.pallas_call(kernel, out_shape=(jax.ShapeDtypeStruct((64, 1024), BF16),...]
where the time goes in v3:
time: 79.7 us; the launch traced here: 78.2 us
  Pallas kernels  74.6 us (94%)
  local copies, waits for them, and re-layouts  2.32 us (3%)
  between operations  1.29 us (2%)
    pallas_call x1, Pallas kernels, on_device(): pl.pallas_call(kernel, out_shape=(jax.ShapeDtypeStruct((64, 1024), BF16),...  74.6 us
    unnamed x4, local copies, waits for them, and re-layouts  2.32 us

profile of v3, /device:TPU:6, one launch (start us, length us, event | category | flops | bytes accessed | tf_op | source)
XLA Modules:
  0.0 78.2 jit_solution(7910202046865161077)
XLA Ops:
  1.3 74.6 %encoder.1 = (bf16[64,1024]{1,0:T(8,128)(2,1)}, bf16[64,2048]{1,0:T(8,128)(2,1)}) custom-call(s32[3]{0:T(128)} %dil_ref.1, s32[1]{0:T(128)S(6)} %copy.13.valid_ref, bf16[32,1024]{1,0:T(8,128)(2,1)} %rec_ref.1, bf16[32,512]{1,0:T(8,128)(2,1)} %bitcast.1, bf16[3,3,64,512]{3,2,1,0:T(8,128)(2,1)} %cw_ref.1, f32[3,64]{1,0:T(4,128)} %cb_ref.1, ...), custom_call_target="tpu_custom_call" | custom-call | tf_op jit(solution)/shard_map/encoder/pallas_call | solution.py:514
  75.9 0.0 copy-start
  75.9 1.6 %copy.14 = bf16[64,1024]{1,0:T(8,128)(2,1)} copy(bf16[64,1024]{1,0:T(8,128)(2,1)} %get-tuple-element.4) | data formatting | bytes 262144
  77.5 0.0 copy-done
  77.5 0.7 copy.15
Async XLA Ops:
  75.9 1.6 %copy-start = (bf16[64,2048]{1,0:T(8,128)(2,1)S(1)}, bf16[64,2048]{1,0:T(8,128)(2,1)}, u32[]{:S(2)}) copy-start(bf16[64,2048]{1,0:T(8,128)(2,1)} %get-tuple-element.5) | copy-start | bytes 786436

commit v4 on v3

--- a/solution.py
+++ b/solution.py
@@ -23,7 +23,7 @@
     dil_ref, valid_ref, rec_ref, sw_ref, cw_ref, cb_ref, kw_ref, vw_ref, q_ref,
     feat_ref, att_ref,
     st, sfull, rec, rwin, wc, bias, kvw, h0, h1, h2, h3, taps, kv, kvall, ka, kt, va, qa,
-    xsend, xlse_send, xrecv, xlse, zsend, zlse_send, zrecv, zlse,
+    score0, score1, xsend, xlse_send, xrecv, xlse, zsend, zlse_send, zrecv, zlse,
     loc, rec_s, rec_r, hal_s, hal_r, b_s, b_r, st_s, st_r, sf_s, sf_r, so_s, so_r,
     y_s, y_r, o_s, o_r, r_s, r_r, c_s, c_r,
     f_s, f_r, kv_s, kv_r, z1, z2, z4,
@@ -76,16 +76,16 @@
     own_rec = rows(32 * s, 32, 32)
     own_out = rows(64 * s, 64, 64)
     local = [
-        pltpu.make_async_copy(cw_ref, wc.at[:, :, own_out, :], loc.at[0]),
-        pltpu.make_async_copy(kw_ref, kvw.at[rows(128 * s, 64, 64)], loc.at[1]),
-        pltpu.make_async_copy(vw_ref, kvw.at[rows(128 * s + 64, 64, 64)], loc.at[2]),
+        pltpu.make_async_copy(cw_ref, wc.at[:, :, :, c, 0], loc.at[0]),
+        pltpu.make_async_copy(kw_ref, kvw.at[0:2, c, 0], loc.at[1]),
+        pltpu.make_async_copy(vw_ref, kvw.at[2:4, c, 0], loc.at[2]),
         pltpu.make_async_copy(q_ref, qa.at[0:64], loc.at[3]),
     ]
     for copy in local:
         copy.start()
     st[own_rec, :] = sw_ref[...]
-    bias[s] = jnp.zeros((8, 128), F32)
-    bias[s, 0:3, 0:64] = cb_ref[...]
+    bias[c, 0] = jnp.zeros((8, 128), F32)
+    bias[c, 0, 0:3, 0:64] = cb_ref[...]
 
     def rec_window(index):
         start = jnp.clip(index - 1, 0, 5)
@@ -125,9 +125,10 @@
         remote(rec_ref.at[:, 0:128], rec.at[own_rec, 384:512], hal_s.at[1], hal_r.at[s], (7, prev_tm)),
     ]
     bias_copies = [
-        same(bias.at[s], b_s.at[n], b_r.at[n], at_y(i, lax.rem(c + k, 2)))
+        remote(bias.at[c, 0], bias.at[c, i], b_s.at[n], b_r.at[n], at_y(i, lax.rem(c + k, 2)))
         for n, (i, k) in enumerate(peers)
     ]
+
     def colour(g):
         return lax.rem(x + 2 * z, 4) if g % 2 == 0 else lax.rem(2 * x + z, 4)
 
@@ -135,82 +136,82 @@
         ways = ((at_x(1), at_x(NX - 1)), (at_z(1), at_z(NZ - 1)))
         return ways if g % 2 == 0 else ways[::-1]
 
-    def piece(g, index, quarter, count=1, lanes=slice(0, 512)):
+    def piece(g, quarter, core, blocks, lanes=slice(0, 512)):
         if g < 3:
-            return wc.at[g, :, rows(64 * index + 16 * quarter, 16 * count, 16), lanes]
-        return kvw.at[rows(128 * index + 32 * quarter, 32 * count, 32), lanes]
+            return wc.at[g, :, quarter, core, blocks, :, lanes]
+        return kvw.at[quarter, core, blocks, :, lanes]
 
     def y_copies(g):
         return [
-            same(piece(g, s, colour(g)), y_s.at[g, i], y_r.at[g, i], at_y(i, c))
+            remote(
+                piece(g, colour(g), c, 0), piece(g, colour(g), c, i),
+                y_s.at[g, i], y_r.at[g, i], at_y(i, c),
+            )
             for i in range(1, NY)
         ]
 
     def own_copy(g):
-        return same(piece(g, s, 0, 4), o_s.at[g], o_r.at[g], sibling)
+        own = wc.at[g, :, :, c, 0] if g < 3 else kvw.at[:, c, 0]
+        return same(own, o_s.at[g], o_r.at[g], sibling)
 
     def issue(g):
         for copy in y_copies(g):
             copy.start()
         own_copy(g).start()
 
-    def relays(g, i):
+    others = slice(1, NY)
+
+    def relays(g):
         (next_full, prev_full), (next_half, prev_half) = along(g)
-        full = piece(g, of_sensor(i), colour(g))
-        low_half = piece(g, of_sensor(i), colour(g), 1, slice(0, 256))
-        high_half = piece(g, of_sensor(i), colour(g), 1, slice(256, 512))
+        full = piece(g, colour(g), c, others)
+        low_half = piece(g, colour(g), c, others, slice(0, 256))
+        high_half = piece(g, colour(g), c, others, slice(256, 512))
         return [
-            same(full, r_s.at[g, i, 0], r_r.at[g, i, 0], next_full),
-            same(full, r_s.at[g, i, 1], r_r.at[g, i, 1], prev_full),
-            same(low_half, r_s.at[g, i, 2], r_r.at[g, i, 2], next_half),
-            same(high_half, r_s.at[g, i, 3], r_r.at[g, i, 3], prev_half),
+            same(full, r_s.at[g, 0], r_r.at[g, 0], next_full),
+            same(full, r_s.at[g, 1], r_r.at[g, 1], prev_full),
+            same(low_half, r_s.at[g, 2], r_r.at[g, 2], next_half),
+            same(high_half, r_s.at[g, 3], r_r.at[g, 3], prev_half),
         ]
 
-    def to_sibling(g, i, k):
+    def to_sibling(g, k):
         quarter = lax.rem(colour(g) + k, 4)
-        return same(piece(g, of_sensor(i), quarter), c_s.at[g, i, k], c_r.at[g, i, k], sibling)
+        return same(piece(g, quarter, c, others), c_s.at[g, k], c_r.at[g, k], sibling)
 
     def forward_y(g):
-        copies = y_copies(g)
-        for i in (1, 3, 2):
-            copies[i - 1].wait_recv()
-            for copy in relays(g, i):
-                copy.start()
-            to_sibling(g, i, 0).start()
+        for copy in y_copies(g):
+            copy.wait_recv()
+        for copy in relays(g):
+            copy.start()
+        to_sibling(g, 0).start()
 
     def forward_relays(g):
-        for i in (1, 3, 2):
-            copies = relays(g, i)
-            copies[0].wait_recv()
-            to_sibling(g, i, 3).start()
-            copies[1].wait_recv()
-            to_sibling(g, i, 1).start()
-            copies[2].wait_recv()
-            copies[3].wait_recv()
-            to_sibling(g, i, 2).start()
+        copies = relays(g)
+        copies[0].wait_recv()
+        to_sibling(g, 3).start()
+        copies[1].wait_recv()
+        to_sibling(g, 1).start()
+        copies[2].wait_recv()
+        copies[3].wait_recv()
+        to_sibling(g, 2).start()
 
     def ready(g):
         own_copy(g).wait_recv()
-        for i in range(1, NY):
-            for k in range(4):
-                to_sibling(g, i, k).wait_recv()
+        for k in range(4):
+            to_sibling(g, k).wait_recv()
 
     def sent(g):
-        for copy in y_copies(g):
+        for copy in y_copies(g) + relays(g):
             copy.wait_send()
         own_copy(g).wait_send()
-        for i in range(1, NY):
-            for copy in relays(g, i):
-                copy.wait_send()
-            for k in range(4):
-                to_sibling(g, i, k).wait_send()
-
+        for k in range(4):
+            to_sibling(g, k).wait_send()
 
     for copy in local:
         copy.wait()
     issue(0)
     for copy in st_y + [st_own] + halo + rec_copies + bias_copies:
         copy.start()
+    issue(1)
 
     first = lax.broadcasted_iota(jnp.int32, (64, LATENTS), 0) == 0
     qa[64:128, :] = jnp.where(first, 1.0, 0.0).astype(BF16)
@@ -225,7 +226,7 @@
         )
 
     forward_y(0)
-    issue(1)
+    issue(2)
     for i in (1, 3, 2):
         st_y[i - 1].wait_recv()
         sib_st(i).start()
@@ -269,15 +270,19 @@
 
     for copy in bias_copies:
         copy.wait_recv()
-    all_bias = jnp.transpose(
-        jnp.concatenate([bias[k][:, 0:64] for k in range(8)], axis=1)
-    )
+    order = [(core, i) for core in range(2) for i in range(NY)]
+    place = [2 * lax.rem(y + NY - i, NY) + core for core, i in order]
+    columns = [jnp.transpose(bias[core, i]) for core, i in order]
 
     def conv(layer, source, target, offset, tiles, start):
         d = dil_ref[layer]
-        for n in range(0, 512, 128):
-            w = wc[layer, :, n : n + 128, :].reshape(384, 512)
+        for q in range(4):
+            w = wc[layer, :, q].reshape(384, 512)
             taps[...] = dot(w, source[...])
+            here = [rows(64 * p + 16 * q, 16, 16) for p in place]
+            old = jnp.concatenate([source[h, :] for h in here], axis=0).astype(F32)
+            col = jnp.concatenate([v[16 * q : 16 * q + 16] for v in columns], axis=0)
+            col = col[:, layer : layer + 1]
             a, b, e = [
                 turned(
                     [taps[128 * j : 128 * j + 128, 128 * k : 128 * k + 128] for k in range(2)],
@@ -285,19 +290,16 @@
                 )
                 for j in range(3)
             ]
-            r = turned(
-                [source[n : n + 128, 128 * k : 128 * k + 128].astype(F32) for k in range(2)],
-                tiles, jnp.int32(offset),
-            )
-            col = all_bias[n : n + 128, layer : layer + 1]
+            r = turned([old[:, 0:128], old[:, 128:256]], tiles, jnp.int32(offset))
             for k in range(tiles):
                 pre = col + a[k] + b[k] + e[k]
                 out = r[k] + 0.5 * pre * (1.0 + lax.erf(pre * 0.7071067811865476))
-                out = jnp.where(inside(128, start + 128 * k), out, 0.0)
-                target[n : n + 128, 128 * k : 128 * k + 128] = out.astype(BF16)
+                out = jnp.where(inside(128, start + 128 * k), out, 0.0).astype(BF16)
+                for n, h in enumerate(here):
+                    target[h, 128 * k : 128 * k + 128] = out[16 * n : 16 * n + 16]
 
     forward_y(1)
-    issue(2)
+    issue(3)
     pl.semaphore_wait(z1.at[0], 1)
     pl.semaphore_wait(z1.at[1], 1)
     signal(z2.at[0], at_z(2))
@@ -306,7 +308,6 @@
     ready(0)
     conv(0, h0, h1, 16, 2, -48)
     forward_y(2)
-    issue(3)
     forward_relays(1)
     pl.semaphore_wait(z2.at[0], 1)
     pl.semaphore_wait(z2.at[1], 1)
@@ -322,8 +323,10 @@
     ready(3)
 
     own_lanes = rows(128 * s, 128, 128)
-    for n in range(0, 1024, 256):
-        kv[n : n + 256, :] = dot(kvw[n : n + 256, :], h3[...]).astype(BF16)
+    for q in range(4):
+        part = dot(kvw[q].reshape(256, 512), h3[...]).astype(BF16)
+        for n, p in enumerate(place):
+            kv[rows(128 * p + 32 * q, 32, 32), :] = part[32 * n : 32 * n + 32]
     kv_copies = []
     feature_copies = []
     for n, (i, k) in enumerate(peers):
@@ -342,8 +345,6 @@
         copy.start()
     kvall[:, own_lanes] = kv[of_head(s), :]
     feat_ref[:, own_lanes] = h3[own_out, :]
-    pl.semaphore_wait(z4.at[0], 1)
-    pl.semaphore_wait(z4.at[1], 1)
     for copy in st_y + [st_own] + rec_copies + halo + bias_copies:
         copy.wait_send()
     for i in range(1, NY):
@@ -356,20 +357,17 @@
     va[0:64, :] = kvall[64:128, :]
     kt[...] = jnp.transpose(ka[...].astype(F32)).astype(BF16)
 
-    def attend(quarter, slot):
-        def block(j, carry):
-            lanes = pl.ds(pl.multiple_of(quarter * QUARTER + j * LB, LB), LB)
-            scores = dot(kt[...], qa[:, lanes])
-            peak = jnp.max(scores, axis=0, keepdims=True)
-            probs = jnp.exp(scores - peak).astype(BF16)
-            both = dot(va[...], probs)
-            total = both[64:65, :]
-            here = pl.ds(pl.multiple_of(j * LB, LB), LB)
-            xsend[slot, :, here] = (both[0:64, :] / total).astype(BF16)
-            xlse_send[slot, :, here] = peak + jnp.log(total)
-            return carry
-
-        lax.fori_loop(0, QUARTER // LB, block, 0)
+    def block_lanes(quarter, j):
+        return pl.ds(pl.multiple_of(quarter * QUARTER + j * LB, LB), LB)
+
+    def finish(scores, slot, j):
+        peak = jnp.max(scores[...], axis=0, keepdims=True)
+        probs = jnp.exp(scores[...] - peak).astype(BF16)
+        both = dot(va[...], probs)
+        total = both[64:65, :]
+        here = slice(j * LB, j * LB + LB)
+        xsend[slot, :, here] = (both[0:64, :] / total).astype(BF16)
+        xlse_send[slot, :, here] = peak + jnp.log(total)
 
     def x_copies(i):
         device = at_x(i)
@@ -382,14 +380,23 @@
                 device_id=device, device_id_type=MESH),
         )
 
-    def peer_quarter(i, carry):
-        attend(lax.rem(x + i, NX), i)
-        for copy in x_copies(i):
-            copy.start()
+    def attend(n, carry):
+        quarter = lax.rem(x + n + 1, NX)
+        slot = lax.rem(n + 1, NX)
+        score1[...] = dot(kt[...], qa[:, block_lanes(quarter, 1)])
+        finish(score0, slot, 0)
+        score0[...] = dot(kt[...], qa[:, block_lanes(lax.rem(quarter + 1, NX), 0)])
+        finish(score1, slot, 1)
+
+        @pl.when(n < NX - 1)
+        def _():
+            for copy in x_copies(n + 1):
+                copy.start()
+
         return carry
 
-    lax.fori_loop(1, NX, peer_quarter, 0)
-    attend(x, 0)
+    score0[...] = dot(kt[...], qa[:, block_lanes(lax.rem(x + 1, NX), 0)])
+    lax.fori_loop(0, NX, attend, 0)
 
     def merge(parts, lses):
         peak = lses[0]
@@ -416,6 +423,9 @@
         zsend[:, lanes] = out.astype(BF16)
         zlse_send[b] = lse
 
+    pl.semaphore_wait(z4.at[0], 1)
+    pl.semaphore_wait(z4.at[1], 1)
+
     def tile_of(zz):
         a, b = zz // 4, lax.rem(zz, 4)
         return pl.ds(pl.multiple_of(16 * a, 16), 16), pl.ds(pl.multiple_of(128 * b, 128), 128), b
@@ -469,29 +479,35 @@
             src_ref=tile, dst_ref=tile, send_sem=as_.at[i], recv_sem=ar.at[i],
             device_id=at_z(i), device_id_type=MESH)
 
-    def spread(zz):
-        tile = att_ref.at[out_tile(zz)]
+    def spread(da):
+        a = lax.rem(z // 4 + da + 4, 4)
+        strip = att_ref.at[
+            pl.ds(pl.multiple_of(16 * a, 16), 16), pl.ds(pl.multiple_of(512 * x, 512), 512)
+        ]
         for i in range(1, NX):
-            remote(tile, tile, bs.at[i], br.at[i], at_x(i)).start()
+            remote(strip, strip, bs.at[i], br.at[i], at_x(i)).start()
 
     def a_start(n, carry):
         a_copy(far_first(n), z).start()
         return carry
 
-    def a_forward(n, carry):
-        i = near_first(n)
-        zz = lax.rem(z + NZ - i, NZ)
+    def a_arrived(i, zz):
         a_copy(i, zz).wait_recv()
-        spread(zz)
-        return carry
 
     def a_done(i, carry):
         a_copy(i, z).wait_send()
         return carry
 
     lax.fori_loop(0, NZ - 1, a_start, 0)
-    spread(z)
-    lax.fori_loop(0, NZ - 1, a_forward, 0)
+    for da in (0, 1, -1, 2):
+        for b in range(4):
+            zz = 4 * lax.rem(z // 4 + da + 4, 4) + b
+            i = lax.rem(z - zz + NZ, NZ)
+            if da == 0:
+                pl.when(i != 0)(lambda: a_arrived(i, zz))
+            else:
+                a_arrived(i, zz)
+        spread(da)
     for i in range(1, NX):
         quarter = att_ref.at[:, pl.ds(pl.multiple_of(512 * x, 512), 512)]
         whole = pltpu.make_async_remote_copy(
@@ -521,16 +537,17 @@
         out_specs=(vmem, vmem),
         scratch_shapes=[
             V((256, 512), BF16), V((512, 256), BF16), V((256, 640), BF16), V((256, 256), BF16),
-            V((3, 3, 512, 512), BF16), V((8, 8, 128), F32), V((1024, 512), BF16),
+            V((3, 3, 4, 2, 4, 16, 512), BF16), V((2, 4, 8, 128), F32), V((4, 2, 4, 32, 512), BF16),
             V((512, 256), BF16), V((512, 256), BF16), V((512, 256), BF16), V((512, 128), BF16),
             V((384, 256), F32), V((1024, 128), BF16), V((128, 1024), BF16),
             V((128, 1024), BF16), V((1024, 128), BF16), V((80, 1024), BF16), V((128, LATENTS), BF16),
+            V((1024, LB), F32), V((1024, LB), F32),
             V((4, 64, 512), BF16), V((4, 1, 512), F32), V((4, 64, 512), BF16), V((4, 1, 512), F32),
             V((64, 512), BF16), V((4, 1, 128), F32), V((16, 16, 128), BF16), V((16, 1, 128), F32),
             dma((4,)), dma((7,)), dma((7,)), dma((2,)), dma((8,)), dma((7,)), dma((7,)),
             dma((4,)), dma((4,)), dma((4,)), dma((4,)), dma, dma,
             dma((4, 4)), dma((4, 4)), dma((4,)), dma((4,)),
-            dma((4, 4, 4)), dma((4, 4, 4)), dma((4, 4, 4)), dma((4, 4, 4)),
+            dma((4, 4)), dma((4, 4)), dma((4, 4)), dma((4, 4)),
             dma((7,)), dma((7,)), dma((7,)), dma((7,)),
             regular((2,)), regular((2,)), regular((2,)),
             dma((4,)), dma((4,)), dma((4,)), dma((4,)),
@@ -541,7 +558,10 @@
             collective_id=0, has_side_effects=True, vmem_limit_bytes=56 * 2**20
         ),
         name="encoder",
-    )(dilations, valid_frames, recording, spatial_w.T, conv_w, conv_b, key_w, value_w, queries)
+    )(
+        dilations, valid_frames, recording, spatial_w.T, conv_w.reshape(3, 3, 4, 16, 512), conv_b,
+        key_w.reshape(2, 32, 512), value_w.reshape(2, 32, 512), queries,
+    )
 
 
 def solution(mesh):

time: 79.7 us -> 76.8 us (0.964)
  Pallas kernels: 74.6 us -> 72 us
    pallas_call x1, Pallas kernels: 74.6 us -> 72 us  [on_device(): pl.pallas_call(kernel, out_shape=(jax.ShapeDtypeStruct((64, 1024), BF16),...]
where the time goes in v4:
time: 76.8 us; the launch traced here: 75.6 us
  Pallas kernels  72 us (94%)
  local copies, waits for them, and re-layouts  2.32 us (3%)
  between operations  1.29 us (2%)
    pallas_call x1, Pallas kernels, on_device(): pl.pallas_call(kernel, out_shape=(jax.ShapeDtypeStruct((64, 1024), BF16),...  72 us
    unnamed x4, local copies, waits for them, and re-layouts  2.32 us

profile of v4, /device:TPU:6, one launch (start us, length us, event | category | flops | bytes accessed | tf_op | source)
XLA Modules:
  0.0 75.6 jit_solution(12443898548942166150)
XLA Ops:
  1.3 72.0 %encoder.1 = (bf16[64,1024]{1,0:T(8,128)(2,1)}, bf16[64,2048]{1,0:T(8,128)(2,1)}) custom-call(s32[3]{0:T(128)} %dil_ref.1, s32[1]{0:T(128)S(6)} %copy.13.valid_ref, bf16[32,1024]{1,0:T(8,128)(2,1)} %rec_ref.1, bf16[32,512]{1,0:T(8,128)(2,1)} %bitcast.7, bf16[3,3,4,16,512]{4,3,2,1,0:T(8,128)(2,1)} %bitcast.4, f32[3,64]{1,0:T(4,128)} %cb_ref.1, ...), custom_call_target="tpu_custom_call" | custom-call | tf_op jit(solution)/shard_map/encoder/pallas_call | solution.py:530
  73.3 0.0 copy-start
  73.3 1.6 %copy.14 = bf16[64,1024]{1,0:T(8,128)(2,1)} copy(bf16[64,1024]{1,0:T(8,128)(2,1)} %get-tuple-element.4) | data formatting | bytes 262144
  74.9 0.0 copy-done
  74.9 0.7 copy.15
Async XLA Ops:
  73.3 1.6 %copy-start = (bf16[64,2048]{1,0:T(8,128)(2,1)S(1)}, bf16[64,2048]{1,0:T(8,128)(2,1)}, u32[]{:S(2)}) copy-start(bf16[64,2048]{1,0:T(8,128)(2,1)} %get-tuple-element.5) | copy-start | bytes 786436

commit v5 on v4

--- a/solution.py
+++ b/solution.py
@@ -277,6 +277,8 @@
     def conv(layer, source, target, offset, tiles, start):
         d = dil_ref[layer]
         for q in range(4):
+            if q == 2:
+                forward_relays(layer + 1)
             w = wc[layer, :, q].reshape(384, 512)
             taps[...] = dot(w, source[...])
             here = [rows(64 * p + 16 * q, 16, 16) for p in place]
@@ -304,22 +306,19 @@
     pl.semaphore_wait(z1.at[1], 1)
     signal(z2.at[0], at_z(2))
     signal(z2.at[1], at_z(NZ - 2))
+    forward_y(2)
     forward_relays(0)
+    forward_y(3)
     ready(0)
     conv(0, h0, h1, 16, 2, -48)
-    forward_y(2)
-    forward_relays(1)
     pl.semaphore_wait(z2.at[0], 1)
     pl.semaphore_wait(z2.at[1], 1)
     signal(z4.at[0], at_z(4))
     signal(z4.at[1], at_z(NZ - 4))
     ready(1)
     conv(1, h1, h2, 16, 2, -32)
-    forward_y(3)
-    forward_relays(2)
     ready(2)
     conv(2, h2, h3, 32, 1, 0)
-    forward_relays(3)
     ready(3)
 
     own_lanes = rows(128 * s, 128, 128)

time: 76.8 us -> 76.5 us (level)
  no operation moved by 1% of the time
where the time goes in v5:
time: 76.5 us; the launch traced here: 75.3 us
  Pallas kernels  71.7 us (94%)
  local copies, waits for them, and re-layouts  2.32 us (3%)
  between operations  1.29 us (2%)
    pallas_call x1, Pallas kernels, on_device(): pl.pallas_call(kernel, out_shape=(jax.ShapeDtypeStruct((64, 1024), BF16),...  71.7 us
    unnamed x4, local copies, waits for them, and re-layouts  2.32 us

profile of v5, /device:TPU:6, one launch (start us, length us, event | category | flops | bytes accessed | tf_op | source)
XLA Modules:
  0.0 75.3 jit_solution(11428582872017850696)
XLA Ops:
  1.3 71.7 %encoder.1 = (bf16[64,1024]{1,0:T(8,128)(2,1)}, bf16[64,2048]{1,0:T(8,128)(2,1)}) custom-call(s32[3]{0:T(128)} %dil_ref.1, s32[1]{0:T(128)S(6)} %copy.13.valid_ref, bf16[32,1024]{1,0:T(8,128)(2,1)} %rec_ref.1, bf16[32,512]{1,0:T(8,128)(2,1)} %bitcast.7, bf16[3,3,4,16,512]{4,3,2,1,0:T(8,128)(2,1)} %bitcast.4, f32[3,64]{1,0:T(4,128)} %cb_ref.1, ...), custom_call_target="tpu_custom_call" | custom-call | tf_op jit(solution)/shard_map/encoder/pallas_call | solution.py:529
  72.9 0.0 copy-start
  72.9 1.6 %copy.14 = bf16[64,1024]{1,0:T(8,128)(2,1)} copy(bf16[64,1024]{1,0:T(8,128)(2,1)} %get-tuple-element.4) | data formatting | bytes 262144
  74.6 0.0 copy-done
  74.6 0.7 copy.15
Async XLA Ops:
  72.9 1.6 %copy-start = (bf16[64,2048]{1,0:T(8,128)(2,1)S(1)}, bf16[64,2048]{1,0:T(8,128)(2,1)}, u32[]{:S(2)}) copy-start(bf16[64,2048]{1,0:T(8,128)(2,1)} %get-tuple-element.5) | copy-start | bytes 786436

commit v6 on v5

--- a/solution.py
+++ b/solution.py
@@ -24,9 +24,8 @@
     feat_ref, att_ref,
     st, sfull, rec, rwin, wc, bias, kvw, h0, h1, h2, h3, taps, kv, kvall, ka, kt, va, qa,
     score0, score1, xsend, xlse_send, xrecv, xlse, zsend, zlse_send, zrecv, zlse,
-    loc, rec_s, rec_r, hal_s, hal_r, b_s, b_r, st_s, st_r, sf_s, sf_r, so_s, so_r,
-    y_s, y_r, o_s, o_r, r_s, r_r, c_s, c_r,
-    f_s, f_r, kv_s, kv_r, z1, z2, z4,
+    loc, rec_s, rec_r, hal_s, hal_r, b_s, b_r, st_s, st_r, sf_s, sf_r,
+    y_s, y_r, r_s, r_r, c_s, c_r, f_s, f_r, kv_s, kv_r, z1, z2, z4,
     xs, xr, xls, xlr, zs, zr, zls, zlr, as_, ar, bs, br,
 ):
     s = lax.axis_index("sensor")
@@ -84,8 +83,8 @@
     for copy in local:
         copy.start()
     st[own_rec, :] = sw_ref[...]
-    bias[c, 0] = jnp.zeros((8, 128), F32)
-    bias[c, 0, 0:3, 0:64] = cb_ref[...]
+    bias[NY * c] = jnp.zeros((8, 128), F32)
+    bias[NY * c, 0:3, 0:64] = cb_ref[...]
 
     def rec_window(index):
         start = jnp.clip(index - 1, 0, 5)
@@ -105,27 +104,30 @@
     def same(ref, ssem, rsem, device):
         return remote(ref, ref, ssem, rsem, device)
 
-    signal(z1.at[0], at_z(1))
-    signal(z1.at[1], at_z(NZ - 1))
+    def drain(sem, ref):
+        pltpu.make_async_copy(ref, ref, sem).wait()
+
+    signal(z1, at_z(1))
+    signal(z1, at_z(NZ - 1))
 
     def of_sensor(i):
         return lax.rem(y + NY - i, NY) * 2 + c
 
-    st_y = [same(st.at[own_rec], st_s.at[i], st_r.at[i], at_y(i, c)) for i in range(1, NY)]
-    st_own = same(st.at[own_rec], so_s, so_r, sibling)
+    st_y = [same(st.at[own_rec], st_s, st_r, at_y(i, c)) for i in range(1, NY)]
+    st_own = same(st.at[own_rec], sf_s, sf_r, sibling)
     rec_copies = []
     for n, (i, k) in enumerate(peers):
         core = lax.rem(c + k, 2)
         src, dst = rec_window(lax.rem(y + i, NY) * 2 + core)
         rec_copies.append(
-            remote(rec_ref.at[:, src], rec.at[own_rec, dst], rec_s.at[n], rec_r.at[n], at_y(i, core))
+            remote(rec_ref.at[:, src], rec.at[own_rec, dst], rec_s, rec_r, at_y(i, core))
         )
     halo = [
-        remote(rec_ref.at[:, 896:1024], rec.at[own_rec, 128:256], hal_s.at[0], hal_r.at[s], (0, next_tm)),
-        remote(rec_ref.at[:, 0:128], rec.at[own_rec, 384:512], hal_s.at[1], hal_r.at[s], (7, prev_tm)),
+        remote(rec_ref.at[:, 896:1024], rec.at[own_rec, 128:256], hal_s, hal_r, (0, next_tm)),
+        remote(rec_ref.at[:, 0:128], rec.at[own_rec, 384:512], hal_s, hal_r, (7, prev_tm)),
     ]
     bias_copies = [
-        remote(bias.at[c, 0], bias.at[c, i], b_s.at[n], b_r.at[n], at_y(i, lax.rem(c + k, 2)))
+        remote(bias.at[NY * c], bias.at[NY * c + i], b_s, b_r, at_y(i, lax.rem(c + k, 2)))
         for n, (i, k) in enumerate(peers)
     ]
 
@@ -145,14 +147,14 @@
         return [
             remote(
                 piece(g, colour(g), c, 0), piece(g, colour(g), c, i),
-                y_s.at[g, i], y_r.at[g, i], at_y(i, c),
+                y_s.at[g], y_r.at[g], at_y(i, c),
             )
             for i in range(1, NY)
         ]
 
     def own_copy(g):
         own = wc.at[g, :, :, c, 0] if g < 3 else kvw.at[:, c, 0]
-        return same(own, o_s.at[g], o_r.at[g], sibling)
+        return same(own, c_s.at[g], c_r.at[g], sibling)
 
     def issue(g):
         for copy in y_copies(g):
@@ -167,44 +169,40 @@
         low_half = piece(g, colour(g), c, others, slice(0, 256))
         high_half = piece(g, colour(g), c, others, slice(256, 512))
         return [
-            same(full, r_s.at[g, 0], r_r.at[g, 0], next_full),
-            same(full, r_s.at[g, 1], r_r.at[g, 1], prev_full),
-            same(low_half, r_s.at[g, 2], r_r.at[g, 2], next_half),
-            same(high_half, r_s.at[g, 3], r_r.at[g, 3], prev_half),
+            same(full, r_s.at[g], r_r.at[g], next_full),
+            same(full, r_s.at[g], r_r.at[g], prev_full),
+            same(low_half, r_s.at[g], r_r.at[g], next_half),
+            same(high_half, r_s.at[g], r_r.at[g], prev_half),
         ]
 
     def to_sibling(g, k):
         quarter = lax.rem(colour(g) + k, 4)
-        return same(piece(g, quarter, c, others), c_s.at[g, k], c_r.at[g, k], sibling)
+        return same(piece(g, quarter, c, others), c_s.at[g], c_r.at[g], sibling)
 
     def forward_y(g):
-        for copy in y_copies(g):
-            copy.wait_recv()
+        drain(y_r.at[g], piece(g, 0, c, others))
         for copy in relays(g):
             copy.start()
         to_sibling(g, 0).start()
 
+    def three_quarters(g):
+        return wc.at[g, :, others, c, others] if g < 3 else kvw.at[others, c, others]
+
     def forward_relays(g):
-        copies = relays(g)
-        copies[0].wait_recv()
-        to_sibling(g, 3).start()
-        copies[1].wait_recv()
-        to_sibling(g, 1).start()
-        copies[2].wait_recv()
-        copies[3].wait_recv()
-        to_sibling(g, 2).start()
+        drain(r_r.at[g], three_quarters(g))
+        for k in (3, 1, 2):
+            to_sibling(g, k).start()
+
+    def core_blocks(g, core):
+        return wc.at[g, :, :, core] if g < 3 else kvw.at[:, core]
 
     def ready(g):
-        own_copy(g).wait_recv()
-        for k in range(4):
-            to_sibling(g, k).wait_recv()
+        drain(c_r.at[g], core_blocks(g, other))
 
     def sent(g):
-        for copy in y_copies(g) + relays(g):
-            copy.wait_send()
-        own_copy(g).wait_send()
-        for k in range(4):
-            to_sibling(g, k).wait_send()
+        drain(y_s.at[g], piece(g, 0, c, others))
+        drain(r_s.at[g], three_quarters(g))
+        drain(c_s.at[g], core_blocks(g, c))
 
     for copy in local:
         copy.wait()
@@ -218,26 +216,23 @@
     va[64:80, :] = jnp.ones((16, 1024), BF16)
     frame = lax.broadcasted_iota(jnp.int32, (64, 1024), 1)
     row = lax.broadcasted_iota(jnp.int32, (64, 1024), 0)
-    ka[64:128, :] = jnp.where((row == 0) & (frame >= valid_ref[0]), -1e30, 0.0).astype(BF16)
+    ka[64:128, :] = jnp.where((row == 0) & (frame >= valid_ref[...]), -1e30, 0.0).astype(BF16)
 
     def sib_st(i):
         return same(
-            st.at[rows(32 * of_sensor(i), 32, 32)], sf_s.at[i], sf_r.at[i], sibling
+            st.at[rows(32 * of_sensor(i), 32, 32)], sf_s, sf_r, sibling
         )
 
     forward_y(0)
     issue(2)
-    for i in (1, 3, 2):
-        st_y[i - 1].wait_recv()
+    drain(st_r, st.at[0:96])
+    for i in range(1, NY):
         sib_st(i).start()
-    for copy in rec_copies:
-        copy.wait_recv()
+    drain(rec_r, rec.at[0:224, 0:384])
 
     @pl.when((s == 0) | (s == 7))
     def _():
-        for k in range(8):
-            tile = rec.at[0:32, 0:128]
-            pltpu.make_async_copy(tile, tile, hal_r.at[k]).wait()
+        drain(hal_r, rec.at[:, 0:128])
 
     def turned(tiles, count, amount):
         lane = lax.broadcasted_iota(jnp.int32, tiles[0].shape, 1)
@@ -260,22 +255,19 @@
         f = lax.broadcasted_iota(jnp.int32, (128, lanes), 1) + start
         return (f >= low) & (f < high)
 
-    st_own.wait_recv()
-    for i in range(1, NY):
-        sib_st(i).wait_recv()
+    drain(sf_r, st.at[0:128])
     sfull[...] = jnp.transpose(st[...].astype(F32)).astype(BF16)
     for n in range(0, 512, 128):
         part = dot(sfull[n : n + 128, :], rwin[...])
         h0[n : n + 128, :] = jnp.where(inside(256, -64), part, 0.0).astype(BF16)
 
-    for copy in bias_copies:
-        copy.wait_recv()
+    drain(b_r, bias.at[1:8])
     order = [(core, i) for core in range(2) for i in range(NY)]
     place = [2 * lax.rem(y + NY - i, NY) + core for core, i in order]
-    columns = [jnp.transpose(bias[core, i]) for core, i in order]
+    columns = [jnp.transpose(bias[NY * core + i]) for core, i in order]
 
     def conv(layer, source, target, offset, tiles, start):
-        d = dil_ref[layer]
+        d = dil_ref[0, layer]
         for q in range(4):
             if q == 2:
                 forward_relays(layer + 1)
@@ -302,19 +294,17 @@
 
     forward_y(1)
     issue(3)
-    pl.semaphore_wait(z1.at[0], 1)
-    pl.semaphore_wait(z1.at[1], 1)
-    signal(z2.at[0], at_z(2))
-    signal(z2.at[1], at_z(NZ - 2))
+    pl.semaphore_wait(z1, 2)
+    signal(z2, at_z(2))
+    signal(z2, at_z(NZ - 2))
     forward_y(2)
     forward_relays(0)
     forward_y(3)
     ready(0)
     conv(0, h0, h1, 16, 2, -48)
-    pl.semaphore_wait(z2.at[0], 1)
-    pl.semaphore_wait(z2.at[1], 1)
-    signal(z4.at[0], at_z(4))
-    signal(z4.at[1], at_z(NZ - 4))
+    pl.semaphore_wait(z2, 2)
+    signal(z4, at_z(4))
+    signal(z4, at_z(NZ - 4))
     ready(1)
     conv(1, h1, h2, 16, 2, -32)
     ready(2)
@@ -332,26 +322,26 @@
         core = lax.rem(c + k, 2)
         to = lax.rem(y + i, NY) * 2 + core
         kv_copies.append(
-            remote(kv.at[of_head(to)], kvall.at[:, own_lanes], kv_s.at[n], kv_r.at[n], at_y(i, core))
+            remote(kv.at[of_head(to)], kvall.at[:, own_lanes], kv_s, kv_r, at_y(i, core))
         )
         feature_copies.append(
             remote(
                 h3.at[rows(64 * to, 64, 64)], feat_ref.at[:, own_lanes],
-                f_s.at[n], f_r.at[n], at_y(i, core),
+                f_s, f_r, at_y(i, core),
             )
         )
     for copy in kv_copies + feature_copies:
         copy.start()
     kvall[:, own_lanes] = kv[of_head(s), :]
     feat_ref[:, own_lanes] = h3[own_out, :]
-    for copy in st_y + [st_own] + rec_copies + halo + bias_copies:
-        copy.wait_send()
-    for i in range(1, NY):
-        sib_st(i).wait_send()
+    drain(st_s, st.at[0:96])
+    drain(sf_s, st.at[0:128])
+    drain(rec_s, rec.at[0:224, 0:384])
+    drain(hal_s, rec.at[0:64, 0:128])
+    drain(b_s, bias.at[1:8])
     for g in range(4):
         sent(g)
-    for copy in kv_copies:
-        copy.wait()
+    drain(kv_r, kvall.at[:, 0:896])
     ka[0:64, :] = (kvall[0:64, :].astype(F32) * 0.125).astype(BF16)
     va[0:64, :] = kvall[64:128, :]
     kt[...] = jnp.transpose(ka[...].astype(F32)).astype(BF16)
@@ -372,10 +362,10 @@
         device = at_x(i)
         return (
             pltpu.make_async_remote_copy(
-                src_ref=xsend.at[i], dst_ref=xrecv.at[i], send_sem=xs.at[i], recv_sem=xr.at[i],
+                src_ref=xsend.at[i], dst_ref=xrecv.at[i], send_sem=xs, recv_sem=xr,
                 device_id=device, device_id_type=MESH),
             pltpu.make_async_remote_copy(
-                src_ref=xlse_send.at[i], dst_ref=xlse.at[i], send_sem=xls.at[i], recv_sem=xlr.at[i],
+                src_ref=xlse_send.at[i], dst_ref=xlse.at[i], send_sem=xls, recv_sem=xlr,
                 device_id=device, device_id_type=MESH),
         )
 
@@ -410,9 +400,8 @@
             out = term if out is None else out + term
         return out / total, peak + jnp.log(total)
 
-    for i in range(1, NX):
-        for copy in x_copies(i):
-            copy.wait()
+    drain(xr, xrecv.at[1:4])
+    drain(xlr, xlse.at[1:4])
     for b in range(4):
         lanes = slice(128 * b, 128 * b + 128)
         out, lse = merge(
@@ -422,8 +411,7 @@
         zsend[:, lanes] = out.astype(BF16)
         zlse_send[b] = lse
 
-    pl.semaphore_wait(z4.at[0], 1)
-    pl.semaphore_wait(z4.at[1], 1)
+    pl.semaphore_wait(z4, 2)
 
     def tile_of(zz):
         a, b = zz // 4, lax.rem(zz, 4)
@@ -434,35 +422,28 @@
         device = at_z(i)
         return (
             pltpu.make_async_remote_copy(
-                src_ref=zsend.at[rows, lanes], dst_ref=zrecv.at[i], send_sem=zs.at[i],
-                recv_sem=zr.at[i], device_id=device, device_id_type=MESH),
+                src_ref=zsend.at[rows, lanes], dst_ref=zrecv.at[i], send_sem=zs,
+                recv_sem=zr, device_id=device, device_id_type=MESH),
             pltpu.make_async_remote_copy(
-                src_ref=zlse_send.at[b], dst_ref=zlse.at[i], send_sem=zls.at[i],
-                recv_sem=zlr.at[i], device_id=device, device_id_type=MESH),
+                src_ref=zlse_send.at[b], dst_ref=zlse.at[i], send_sem=zls,
+                recv_sem=zlr, device_id=device, device_id_type=MESH),
         )
 
     def far_first(n):
         k = (n + 1) // 2
         return 8 + k * (1 - 2 * lax.rem(n, 2))
-
-    def near_first(n):
-        return far_first(14 - n)
 
     def z_start(n, carry):
         for copy in z_copies(far_first(n)):
             copy.start()
         return carry
 
-    def z_wait(n, carry):
-        for copy in z_copies(near_first(n)):
-            copy.wait()
-        return carry
-
     lax.fori_loop(0, NZ - 1, z_start, 0)
     my_rows, my_lanes, my_b = tile_of(z)
     zrecv[0] = zsend[my_rows, my_lanes]
     zlse[0] = zlse_send[my_b]
-    lax.fori_loop(0, NZ - 1, z_wait, 0)
+    drain(zr, zrecv.at[1:16])
+    drain(zlr, zlse.at[1:16])
     out, _ = merge([zrecv[i] for i in range(NZ)], [zlse[i] for i in range(NZ)])
 
     def out_tile(zz):
@@ -475,7 +456,7 @@
     def a_copy(i, zz):
         tile = att_ref.at[out_tile(zz)]
         return pltpu.make_async_remote_copy(
-            src_ref=tile, dst_ref=tile, send_sem=as_.at[i], recv_sem=ar.at[i],
+            src_ref=tile, dst_ref=tile, send_sem=as_, recv_sem=ar.at[zz // 4],
             device_id=at_z(i), device_id_type=MESH)
 
     def spread(da):
@@ -484,83 +465,81 @@
             pl.ds(pl.multiple_of(16 * a, 16), 16), pl.ds(pl.multiple_of(512 * x, 512), 512)
         ]
         for i in range(1, NX):
-            remote(strip, strip, bs.at[i], br.at[i], at_x(i)).start()
+            remote(strip, strip, bs, br, at_x(i)).start()
 
     def a_start(n, carry):
         a_copy(far_first(n), z).start()
         return carry
 
-    def a_arrived(i, zz):
-        a_copy(i, zz).wait_recv()
-
-    def a_done(i, carry):
-        a_copy(i, z).wait_send()
-        return carry
-
     lax.fori_loop(0, NZ - 1, a_start, 0)
     for da in (0, 1, -1, 2):
-        for b in range(4):
-            zz = 4 * lax.rem(z // 4 + da + 4, 4) + b
-            i = lax.rem(z - zz + NZ, NZ)
-            if da == 0:
-                pl.when(i != 0)(lambda: a_arrived(i, zz))
-            else:
-                a_arrived(i, zz)
+        strip = zsend.at[0:16, 0 : 384 if da == 0 else 512]
+        drain(ar.at[lax.rem(z // 4 + da + 4, 4)], strip)
         spread(da)
-    for i in range(1, NX):
-        quarter = att_ref.at[:, pl.ds(pl.multiple_of(512 * x, 512), 512)]
-        whole = pltpu.make_async_remote_copy(
-            src_ref=quarter, dst_ref=quarter, send_sem=bs.at[i], recv_sem=br.at[i],
-            device_id=at_x(i), device_id_type=MESH)
-        whole.wait_recv()
-        whole.wait_send()
-    lax.fori_loop(1, NZ, a_done, 0)
-    for copy in feature_copies:
+    drain(br, xrecv.at[1:4])
+    drain(bs, xrecv.at[1:4])
+    drain(as_, zrecv.at[1:16])
+    drain(zs, zrecv.at[1:16])
+    drain(zls, zlse.at[1:16])
+    drain(xs, xrecv.at[1:4])
+    drain(xls, xlse.at[1:4])
+    drain(kv_s, kvall.at[:, 0:896])
+    drain(f_s, h3.at[0:448])
+    drain(f_r, h3.at[0:448])
+
+
+def hand_on(feat, att, feat_out, att_out, sem_f, sem_a):
+    copies = [pltpu.make_async_copy(feat, feat_out, sem_f), pltpu.make_async_copy(att, att_out, sem_a)]
+    for copy in copies:
+        copy.start()
+    for copy in copies:
         copy.wait()
 
 
 def on_device(recording, spatial_w, conv_w, conv_b, dilations, valid_frames, key_w, value_w, queries):
     vmem = pl.BlockSpec(memory_space=pltpu.VMEM)
-    smem = pl.BlockSpec(memory_space=pltpu.SMEM)
     hbm = pl.BlockSpec(memory_space=pl.ANY)
     dma = pltpu.SemaphoreType.DMA
     regular = pltpu.SemaphoreType.REGULAR
     V = pltpu.VMEM
-    return pl.pallas_call(
+    results = pl.pallas_call(
         kernel,
         out_shape=(
             jax.ShapeDtypeStruct((64, 1024), BF16),
             jax.ShapeDtypeStruct((64, LATENTS), BF16),
         ),
-        in_specs=[smem, smem, vmem, vmem, hbm, vmem, hbm, hbm, hbm],
+        in_specs=[vmem, vmem, vmem, vmem, hbm, vmem, hbm, hbm, hbm],
         out_specs=(vmem, vmem),
         scratch_shapes=[
             V((256, 512), BF16), V((512, 256), BF16), V((256, 640), BF16), V((256, 256), BF16),
-            V((3, 3, 4, 2, 4, 16, 512), BF16), V((2, 4, 8, 128), F32), V((4, 2, 4, 32, 512), BF16),
+            V((3, 3, 4, 2, 4, 16, 512), BF16), V((8, 8, 128), F32), V((4, 2, 4, 32, 512), BF16),
             V((512, 256), BF16), V((512, 256), BF16), V((512, 256), BF16), V((512, 128), BF16),
             V((384, 256), F32), V((1024, 128), BF16), V((128, 1024), BF16),
             V((128, 1024), BF16), V((1024, 128), BF16), V((80, 1024), BF16), V((128, LATENTS), BF16),
             V((1024, LB), F32), V((1024, LB), F32),
             V((4, 64, 512), BF16), V((4, 1, 512), F32), V((4, 64, 512), BF16), V((4, 1, 512), F32),
             V((64, 512), BF16), V((4, 1, 128), F32), V((16, 16, 128), BF16), V((16, 1, 128), F32),
-            dma((4,)), dma((7,)), dma((7,)), dma((2,)), dma((8,)), dma((7,)), dma((7,)),
-            dma((4,)), dma((4,)), dma((4,)), dma((4,)), dma, dma,
-            dma((4, 4)), dma((4, 4)), dma((4,)), dma((4,)),
-            dma((4, 4)), dma((4, 4)), dma((4, 4)), dma((4, 4)),
-            dma((7,)), dma((7,)), dma((7,)), dma((7,)),
-            regular((2,)), regular((2,)), regular((2,)),
-            dma((4,)), dma((4,)), dma((4,)), dma((4,)),
-            dma((16,)), dma((16,)), dma((16,)), dma((16,)),
-            dma((16,)), dma((16,)), dma((4,)), dma((4,)),
+            dma((4,)), dma, dma, dma, dma, dma, dma, dma, dma, dma, dma,
+            dma((4,)), dma((4,)), dma((4,)), dma((4,)), dma((4,)), dma((4,)),
+            dma, dma, dma, dma, regular, regular, regular,
+            dma, dma, dma, dma, dma, dma, dma, dma, dma, dma((4,)), dma, dma,
         ],
         compiler_params=pltpu.CompilerParams(
             collective_id=0, has_side_effects=True, vmem_limit_bytes=56 * 2**20
         ),
         name="encoder",
     )(
-        dilations, valid_frames, recording, spatial_w.T, conv_w.reshape(3, 3, 4, 16, 512), conv_b,
+        dilations.reshape(1, 3), valid_frames.reshape(1, 1), recording, spatial_w.T, conv_w.reshape(3, 3, 4, 16, 512), conv_b,
         key_w.reshape(2, 32, 512), value_w.reshape(2, 32, 512), queries,
     )
+    return pl.pallas_call(
+        hand_on,
+        out_shape=tuple(jax.ShapeDtypeStruct(r.shape, r.dtype) for r in results),
+        in_specs=[hbm, hbm],
+        out_specs=(hbm, hbm),
+        scratch_shapes=[dma, dma],
+        name="hand_on",
+    )(*results)
 
 
 def solution(mesh):

time: 76.5 us -> 84.2 us (1.10)
  Pallas kernels: 71.7 us -> 82 us
  local copies, waits for them, and re-layouts: 2.32 us -> 0 us
    pallas_call x0 -> x1, Pallas kernels: none -> 13 us  [on_device(): pl.pallas_call(hand_on, out_shape=tuple((jax.ShapeDtypeStruct(r.shape, r....]
    pallas_call x1, Pallas kernels: 71.7 us -> 69 us  [on_device(): pl.pallas_call(kernel, out_shape=(jax.ShapeDtypeStruct((64, 1024), BF16),...]
    unnamed x4 -> x0, local copies, waits for them, and re-layouts: 2.32 us -> none
where the time goes in v6:
time: 84.2 us; the launch traced here: 83.3 us
  Pallas kernels  82 us (97%)
  between operations  1.29 us (2%)
    pallas_call x1, Pallas kernels, on_device(): pl.pallas_call(kernel, out_shape=(jax.ShapeDtypeStruct((64, 1024), BF16),...  69 us
    pallas_call x1, Pallas kernels, on_device(): pl.pallas_call(hand_on, out_shape=tuple((jax.ShapeDtypeStruct(r.shape, r....  13 us

profile of v6, /device:TPU:6, one launch (start us, length us, event | category | flops | bytes accessed | tf_op | source)
XLA Modules:
  0.0 83.3 jit_solution(11861041224471769794)
XLA Ops:
  1.3 69.0 %encoder.1 = (bf16[64,1024]{1,0:T(8,128)(2,1)}, bf16[64,2048]{1,0:T(8,128)(2,1)}) custom-call(s32[1,3]{1,0:T(1,128)} %bitcast.11, s32[1,1]{1,0:T(1,128)} %bitcast.6.valid_ref, bf16[32,1024]{1,0:T(8,128)(2,1)} %rec_ref.1, bf16[32,512]{1,0:T(8,128)(2,1)} %bitcast.10, bf16[3,3,4,16,512]{4,3,2,1,0:T(8,128)(2,1)} %bitcast.7, f32[3,64]{1,0:T(4,128)} %cb_ref.1, ...), custom_call_target="tpu_custom_call" | custom-call | tf_op jit(solution)/shard_map/encoder/pallas_call | solution.py:505
  70.3 13.0 %hand_on.1 = (bf16[64,1024]{1,0:T(8,128)(2,1)}, bf16[64,2048]{1,0:T(8,128)(2,1)}) custom-call(bf16[64,1024]{1,0:T(8,128)(2,1)} %get-tuple-element.4.feat, bf16[64,2048]{1,0:T(8,128)(2,1)} %get-tuple-element.5.att), custom_call_target="tpu_custom_call" | custom-call | tf_op jit(solution)/shard_map/hand_on/pallas_call | solution.py:535

commit v7 on v6

--- a/solution.py
+++ b/solution.py
@@ -330,7 +330,7 @@
                 f_s, f_r, at_y(i, core),
             )
         )
-    for copy in kv_copies + feature_copies:
+    for copy in kv_copies:
         copy.start()
     kvall[:, own_lanes] = kv[of_head(s), :]
     feat_ref[:, own_lanes] = h3[own_out, :]
@@ -342,6 +342,8 @@
     for g in range(4):
         sent(g)
     drain(kv_r, kvall.at[:, 0:896])
+    for copy in feature_copies:
+        copy.start()
     ka[0:64, :] = (kvall[0:64, :].astype(F32) * 0.125).astype(BF16)
     va[0:64, :] = kvall[64:128, :]
     kt[...] = jnp.transpose(ka[...].astype(F32)).astype(BF16)
@@ -488,12 +490,9 @@
     drain(f_r, h3.at[0:448])
 
 
-def hand_on(feat, att, feat_out, att_out, sem_f, sem_a):
-    copies = [pltpu.make_async_copy(feat, feat_out, sem_f), pltpu.make_async_copy(att, att_out, sem_a)]
-    for copy in copies:
-        copy.start()
-    for copy in copies:
-        copy.wait()
+def hand_on(feat, att, feat_out, att_out):
+    feat_out[...] = feat[...]
+    att_out[...] = att[...]
 
 
 def on_device(recording, spatial_w, conv_w, conv_b, dilations, valid_frames, key_w, value_w, queries):
@@ -535,9 +534,8 @@
     return pl.pallas_call(
         hand_on,
         out_shape=tuple(jax.ShapeDtypeStruct(r.shape, r.dtype) for r in results),
-        in_specs=[hbm, hbm],
-        out_specs=(hbm, hbm),
-        scratch_shapes=[dma, dma],
+        in_specs=[vmem, vmem],
+        out_specs=(vmem, vmem),
         name="hand_on",
     )(*results)
 

time: 84.2 us -> 72.2 us (0.86)
  Pallas kernels: 82 us -> 70.7 us
    pallas_call x1, Pallas kernels: 13 us -> 1.78 us  [on_device(): pl.pallas_call(hand_on, out_shape=tuple((jax.ShapeDtypeStruct(r.shape, r....]
where the time goes in v7:
time: 72.2 us; the launch traced here: 72 us
  Pallas kernels  70.7 us (98%)
  between operations  1.29 us (2%)
    pallas_call x1, Pallas kernels, on_device(): pl.pallas_call(kernel, out_shape=(jax.ShapeDtypeStruct((64, 1024), BF16),...  68.9 us
    pallas_call x1, Pallas kernels, on_device(): pl.pallas_call(hand_on, out_shape=tuple((jax.ShapeDtypeStruct(r.shape, r....  1.78 us

profile of v7, /device:TPU:6, one launch (start us, length us, event | category | flops | bytes accessed | tf_op | source)
XLA Modules:
  0.0 72.0 jit_solution(10335948719124229293)
XLA Ops:
  1.3 68.9 %encoder.1 = (bf16[64,1024]{1,0:T(8,128)(2,1)}, bf16[64,2048]{1,0:T(8,128)(2,1)}) custom-call(s32[1,3]{1,0:T(1,128)} %bitcast.11, s32[1,1]{1,0:T(1,128)} %bitcast.6.valid_ref, bf16[32,1024]{1,0:T(8,128)(2,1)} %rec_ref.1, bf16[32,512]{1,0:T(8,128)(2,1)} %bitcast.10, bf16[3,3,4,16,512]{4,3,2,1,0:T(8,128)(2,1)} %bitcast.7, f32[3,64]{1,0:T(4,128)} %cb_ref.1, ...), custom_call_target="tpu_custom_call" | custom-call | tf_op jit(solution)/shard_map/encoder/pallas_call | solution.py:504
  70.2 1.8 %hand_on.1 = (bf16[64,1024]{1,0:T(8,128)(2,1)}, bf16[64,2048]{1,0:T(8,128)(2,1)}) custom-call(bf16[64,1024]{1,0:T(8,128)(2,1)} %get-tuple-element.4.feat, bf16[64,2048]{1,0:T(8,128)(2,1)} %get-tuple-element.5.att), custom_call_target="tpu_custom_call" | custom-call | tf_op jit(solution)/shard_map/hand_on/pallas_call | solution.py:534

commit v8 on v7

--- a/solution.py
+++ b/solution.py
@@ -206,10 +206,10 @@
 
     for copy in local:
         copy.wait()
-    issue(0)
+    for g in range(4):
+        issue(g)
     for copy in st_y + [st_own] + halo + rec_copies + bias_copies:
         copy.start()
-    issue(1)
 
     first = lax.broadcasted_iota(jnp.int32, (64, LATENTS), 0) == 0
     qa[64:128, :] = jnp.where(first, 1.0, 0.0).astype(BF16)
@@ -224,10 +224,17 @@
         )
 
     forward_y(0)
-    issue(2)
+    forward_y(1)
+    forward_y(2)
+    forward_relays(0)
+    forward_y(3)
+    pl.semaphore_wait(z1, 2)
+    signal(z2, at_z(2))
+    signal(z2, at_z(NZ - 2))
     drain(st_r, st.at[0:96])
     for i in range(1, NY):
         sib_st(i).start()
+    forward_relays(1)
     drain(rec_r, rec.at[0:224, 0:384])
 
     @pl.when((s == 0) | (s == 7))
@@ -266,11 +273,11 @@
     place = [2 * lax.rem(y + NY - i, NY) + core for core, i in order]
     columns = [jnp.transpose(bias[NY * core + i]) for core, i in order]
 
-    def conv(layer, source, target, offset, tiles, start):
+    def conv(layer, source, target, offset, tiles, start, forwarded=None):
         d = dil_ref[0, layer]
         for q in range(4):
-            if q == 2:
-                forward_relays(layer + 1)
+            if q == 2 and forwarded is not None:
+                forward_relays(forwarded)
             w = wc[layer, :, q].reshape(384, 512)
             taps[...] = dot(w, source[...])
             here = [rows(64 * p + 16 * q, 16, 16) for p in place]
@@ -292,16 +299,9 @@
                 for n, h in enumerate(here):
                     target[h, 128 * k : 128 * k + 128] = out[16 * n : 16 * n + 16]
 
-    forward_y(1)
-    issue(3)
-    pl.semaphore_wait(z1, 2)
-    signal(z2, at_z(2))
-    signal(z2, at_z(NZ - 2))
-    forward_y(2)
-    forward_relays(0)
-    forward_y(3)
+    forward_relays(2)
     ready(0)
-    conv(0, h0, h1, 16, 2, -48)
+    conv(0, h0, h1, 16, 2, -48, 3)
     pl.semaphore_wait(z2, 2)
     signal(z4, at_z(4))
     signal(z4, at_z(NZ - 4))
@@ -371,23 +371,18 @@
                 device_id=device, device_id_type=MESH),
         )
 
-    def attend(n, carry):
+    score0[...] = dot(kt[...], qa[:, block_lanes(lax.rem(x + 1, NX), 0)])
+    for n in range(NX):
+        slot = (n + 1) % NX
         quarter = lax.rem(x + n + 1, NX)
-        slot = lax.rem(n + 1, NX)
         score1[...] = dot(kt[...], qa[:, block_lanes(quarter, 1)])
         finish(score0, slot, 0)
-        score0[...] = dot(kt[...], qa[:, block_lanes(lax.rem(quarter + 1, NX), 0)])
+        if n < NX - 1:
+            score0[...] = dot(kt[...], qa[:, block_lanes(lax.rem(quarter + 1, NX), 0)])
         finish(score1, slot, 1)
-
-        @pl.when(n < NX - 1)
-        def _():
-            for copy in x_copies(n + 1):
+        if n < NX - 1:
+            for copy in x_copies(slot):
                 copy.start()
-
-        return carry
-
-    score0[...] = dot(kt[...], qa[:, block_lanes(lax.rem(x + 1, NX), 0)])
-    lax.fori_loop(0, NX, attend, 0)
 
     def merge(parts, lses):
         peak = lses[0]

time: 72.2 us -> 67.9 us (0.940)
  Pallas kernels: 70.7 us -> 65.7 us
    pallas_call x1, Pallas kernels: 68.9 us -> 64 us  [on_device(): pl.pallas_call(kernel, out_shape=(jax.ShapeDtypeStruct((64, 1024), BF16),...]
where the time goes in v8:
time: 67.9 us; the launch traced here: 67 us
  Pallas kernels  65.7 us (97%)
  between operations  1.29 us (2%)
    pallas_call x1, Pallas kernels, on_device(): pl.pallas_call(kernel, out_shape=(jax.ShapeDtypeStruct((64, 1024), BF16),...  64 us
    pallas_call x1, Pallas kernels, on_device(): pl.pallas_call(hand_on, out_shape=tuple((jax.ShapeDtypeStruct(r.shape, r....  1.78 us

profile of v8, /device:TPU:6, one launch (start us, length us, event | category | flops | bytes accessed | tf_op | source)
XLA Modules:
  0.0 67.0 jit_solution(10005629817370751671)
XLA Ops:
  1.3 64.0 %encoder.1 = (bf16[64,1024]{1,0:T(8,128)(2,1)}, bf16[64,2048]{1,0:T(8,128)(2,1)}) custom-call(s32[1,3]{1,0:T(1,128)} %bitcast.11, s32[1,1]{1,0:T(1,128)} %bitcast.6.valid_ref, bf16[32,1024]{1,0:T(8,128)(2,1)} %rec_ref.1, bf16[32,512]{1,0:T(8,128)(2,1)} %bitcast.10, bf16[3,3,4,16,512]{4,3,2,1,0:T(8,128)(2,1)} %bitcast.7, f32[3,64]{1,0:T(4,128)} %cb_ref.1, ...), custom_call_target="tpu_custom_call" | custom-call | tf_op jit(solution)/shard_map/encoder/pallas_call | solution.py:499
  65.2 1.8 %hand_on.1 = (bf16[64,1024]{1,0:T(8,128)(2,1)}, bf16[64,2048]{1,0:T(8,128)(2,1)}) custom-call(bf16[64,1024]{1,0:T(8,128)(2,1)} %get-tuple-element.4.feat, bf16[64,2048]{1,0:T(8,128)(2,1)} %get-tuple-element.5.att), custom_call_target="tpu_custom_call" | custom-call | tf_op jit(solution)/shard_map/hand_on/pallas_call | solution.py:529

commit v9 on v8

--- a/solution.py
+++ b/solution.py
@@ -24,7 +24,7 @@
     feat_ref, att_ref,
     st, sfull, rec, rwin, wc, bias, kvw, h0, h1, h2, h3, taps, kv, kvall, ka, kt, va, qa,
     score0, score1, xsend, xlse_send, xrecv, xlse, zsend, zlse_send, zrecv, zlse,
-    loc, rec_s, rec_r, hal_s, hal_r, b_s, b_r, st_s, st_r, sf_s, sf_r,
+    loc, rec_s, rec_r, hal_s, hal_r, b_s, b_r,
     y_s, y_r, r_s, r_r, c_s, c_r, f_s, f_r, kv_s, kv_r, z1, z2, z4,
     xs, xr, xls, xlr, zs, zr, zls, zlr, as_, ar, bs, br,
 ):
@@ -72,7 +72,6 @@
     def of_head(index):
         return rows(128 * index, 128, 128)
 
-    own_rec = rows(32 * s, 32, 32)
     own_out = rows(64 * s, 64, 64)
     local = [
         pltpu.make_async_copy(cw_ref, wc.at[:, :, :, c, 0], loc.at[0]),
@@ -82,7 +81,7 @@
     ]
     for copy in local:
         copy.start()
-    st[own_rec, :] = sw_ref[...]
+    st[NY * c] = sw_ref[...]
     bias[NY * c] = jnp.zeros((8, 128), F32)
     bias[NY * c, 0:3, 0:64] = cb_ref[...]
 
@@ -91,7 +90,7 @@
         return rows(128 * start, 384, 128), rows(128 * (start - index + 2), 384, 128)
 
     here_src, here_dst = rec_window(s)
-    rec[own_rec, here_dst] = rec_ref[:, here_src]
+    rec[NY * c, :, here_dst] = rec_ref[:, here_src]
 
     pl.semaphore_wait(barrier, 7 + 3 + 2 + 2)
 
@@ -110,27 +109,24 @@
     signal(z1, at_z(1))
     signal(z1, at_z(NZ - 1))
 
-    def of_sensor(i):
-        return lax.rem(y + NY - i, NY) * 2 + c
-
-    st_y = [same(st.at[own_rec], st_s, st_r, at_y(i, c)) for i in range(1, NY)]
-    st_own = same(st.at[own_rec], sf_s, sf_r, sibling)
     rec_copies = []
     for n, (i, k) in enumerate(peers):
         core = lax.rem(c + k, 2)
         src, dst = rec_window(lax.rem(y + i, NY) * 2 + core)
         rec_copies.append(
-            remote(rec_ref.at[:, src], rec.at[own_rec, dst], rec_s, rec_r, at_y(i, core))
+            remote(rec_ref.at[:, src], rec.at[NY * c + i, :, dst], rec_s, rec_r, at_y(i, core))
         )
     halo = [
-        remote(rec_ref.at[:, 896:1024], rec.at[own_rec, 128:256], hal_s, hal_r, (0, next_tm)),
-        remote(rec_ref.at[:, 0:128], rec.at[own_rec, 384:512], hal_s, hal_r, (7, prev_tm)),
+        remote(rec_ref.at[:, 896:1024], rec.at[NY * c + lax.rem(NY - y, NY), :, 128:256], hal_s, hal_r, (0, next_tm)),
+        remote(rec_ref.at[:, 0:128], rec.at[NY * c + NY - 1 - y, :, 384:512], hal_s, hal_r, (7, prev_tm)),
     ]
     bias_copies = [
         remote(bias.at[NY * c], bias.at[NY * c + i], b_s, b_r, at_y(i, lax.rem(c + k, 2)))
         for n, (i, k) in enumerate(peers)
     ]
 
+    others = slice(1, NY)
+
     def colour(g):
         return lax.rem(x + 2 * z, 4) if g % 2 == 0 else lax.rem(2 * x + z, 4)
 
@@ -138,10 +134,18 @@
         ways = ((at_x(1), at_x(NX - 1)), (at_z(1), at_z(NZ - 1)))
         return ways if g % 2 == 0 else ways[::-1]
 
-    def piece(g, quarter, core, blocks, lanes=slice(0, 512)):
-        if g < 3:
-            return wc.at[g, :, quarter, core, blocks, :, lanes]
-        return kvw.at[quarter, core, blocks, :, lanes]
+    def piece(g, quarter, core, blocks, half=None):
+        if g == 4:
+            if blocks == others:
+                blocks = pl.ds(NY * core + 1, NY - 1)
+            else:
+                blocks = NY * core + blocks
+            part = slice(0, 32) if half is None else slice(16 * half, 16 * half + 16)
+            return st.at[blocks, part, rows(128 * quarter, 128, 128)]
+        lanes = slice(0, 512) if half is None else slice(256 * half, 256 * half + 256)
+        if g == 3:
+            return kvw.at[quarter, core, blocks, :, lanes]
+        return wc.at[g, :, quarter, core, blocks, :, lanes]
 
     def y_copies(g):
         return [
@@ -153,7 +157,7 @@
         ]
 
     def own_copy(g):
-        own = wc.at[g, :, :, c, 0] if g < 3 else kvw.at[:, c, 0]
+        own = st.at[NY * c] if g == 4 else kvw.at[:, c, 0] if g == 3 else wc.at[g, :, :, c, 0]
         return same(own, c_s.at[g], c_r.at[g], sibling)
 
     def issue(g):
@@ -161,13 +165,11 @@
             copy.start()
         own_copy(g).start()
 
-    others = slice(1, NY)
-
     def relays(g):
         (next_full, prev_full), (next_half, prev_half) = along(g)
         full = piece(g, colour(g), c, others)
-        low_half = piece(g, colour(g), c, others, slice(0, 256))
-        high_half = piece(g, colour(g), c, others, slice(256, 512))
+        low_half = piece(g, colour(g), c, others, 0)
+        high_half = piece(g, colour(g), c, others, 1)
         return [
             same(full, r_s.at[g], r_r.at[g], next_full),
             same(full, r_s.at[g], r_r.at[g], prev_full),
@@ -186,7 +188,9 @@
         to_sibling(g, 0).start()
 
     def three_quarters(g):
-        return wc.at[g, :, others, c, others] if g < 3 else kvw.at[others, c, others]
+        if g == 4:
+            return st.at[0:3, :, 0:384]
+        return kvw.at[others, c, others] if g == 3 else wc.at[g, :, others, c, others]
 
     def forward_relays(g):
         drain(r_r.at[g], three_quarters(g))
@@ -194,7 +198,9 @@
             to_sibling(g, k).start()
 
     def core_blocks(g, core):
-        return wc.at[g, :, :, core] if g < 3 else kvw.at[:, core]
+        if g == 4:
+            return st.at[0:4]
+        return kvw.at[:, core] if g == 3 else wc.at[g, :, :, core]
 
     def ready(g):
         drain(c_r.at[g], core_blocks(g, other))
@@ -206,9 +212,9 @@
 
     for copy in local:
         copy.wait()
-    for g in range(4):
+    for g in (4, 0, 1, 2, 3):
         issue(g)
-    for copy in st_y + [st_own] + halo + rec_copies + bias_copies:
+    for copy in halo + rec_copies + bias_copies:
         copy.start()
 
     first = lax.broadcasted_iota(jnp.int32, (64, LATENTS), 0) == 0
@@ -218,28 +224,22 @@
     row = lax.broadcasted_iota(jnp.int32, (64, 1024), 0)
     ka[64:128, :] = jnp.where((row == 0) & (frame >= valid_ref[...]), -1e30, 0.0).astype(BF16)
 
-    def sib_st(i):
-        return same(
-            st.at[rows(32 * of_sensor(i), 32, 32)], sf_s, sf_r, sibling
-        )
-
+    forward_y(4)
     forward_y(0)
     forward_y(1)
+    forward_relays(4)
     forward_y(2)
     forward_relays(0)
     forward_y(3)
     pl.semaphore_wait(z1, 2)
     signal(z2, at_z(2))
     signal(z2, at_z(NZ - 2))
-    drain(st_r, st.at[0:96])
-    for i in range(1, NY):
-        sib_st(i).start()
     forward_relays(1)
-    drain(rec_r, rec.at[0:224, 0:384])
+    drain(rec_r, rec.at[0:7, :, 0:384])
 
     @pl.when((s == 0) | (s == 7))
     def _():
-        drain(hal_r, rec.at[:, 0:128])
+        drain(hal_r, rec.at[:, :, 0:128])
 
     def turned(tiles, count, amount):
         lane = lax.broadcasted_iota(jnp.int32, tiles[0].shape, 1)
@@ -250,7 +250,7 @@
         return [jnp.where(keep, rolled[k], rolled[min(k + 1, last)]) for k in range(count)]
 
     window = turned(
-        [rec[:, 128 * k : 128 * k + 128].astype(F32) for k in range(1, 4)], 2, jnp.int32(64)
+        [rec[:, :, 128 * k : 128 * k + 128].reshape(256, 128).astype(F32) for k in range(1, 4)], 2, jnp.int32(64)
     )
     for k in range(2):
         rwin[:, 128 * k : 128 * k + 128] = window[k].astype(BF16)
@@ -262,8 +262,8 @@
         f = lax.broadcasted_iota(jnp.int32, (128, lanes), 1) + start
         return (f >= low) & (f < high)
 
-    drain(sf_r, st.at[0:128])
-    sfull[...] = jnp.transpose(st[...].astype(F32)).astype(BF16)
+    ready(4)
+    sfull[...] = jnp.transpose(st[...].reshape(256, 512).astype(F32)).astype(BF16)
     for n in range(0, 512, 128):
         part = dot(sfull[n : n + 128, :], rwin[...])
         h0[n : n + 128, :] = jnp.where(inside(256, -64), part, 0.0).astype(BF16)
@@ -279,14 +279,15 @@
             if q == 2 and forwarded is not None:
                 forward_relays(forwarded)
             w = wc[layer, :, q].reshape(384, 512)
-            taps[...] = dot(w, source[...])
+            tap = taps.at[q % 2]
+            tap[...] = dot(w, source[...])
             here = [rows(64 * p + 16 * q, 16, 16) for p in place]
             old = jnp.concatenate([source[h, :] for h in here], axis=0).astype(F32)
             col = jnp.concatenate([v[16 * q : 16 * q + 16] for v in columns], axis=0)
             col = col[:, layer : layer + 1]
             a, b, e = [
                 turned(
-                    [taps[128 * j : 128 * j + 128, 128 * k : 128 * k + 128] for k in range(2)],
+                    [tap[128 * j : 128 * j + 128, 128 * k : 128 * k + 128] for k in range(2)],
                     tiles, offset + (j - 1) * d,
                 )
                 for j in range(3)
@@ -334,12 +335,10 @@
         copy.start()
     kvall[:, own_lanes] = kv[of_head(s), :]
     feat_ref[:, own_lanes] = h3[own_out, :]
-    drain(st_s, st.at[0:96])
-    drain(sf_s, st.at[0:128])
-    drain(rec_s, rec.at[0:224, 0:384])
-    drain(hal_s, rec.at[0:64, 0:128])
+    drain(rec_s, rec.at[0:7, :, 0:384])
+    drain(hal_s, rec.at[0:2, :, 0:128])
     drain(b_s, bias.at[1:8])
-    for g in range(4):
+    for g in range(5):
         sent(g)
     drain(kv_r, kvall.at[:, 0:896])
     for copy in feature_copies:
@@ -505,16 +504,16 @@
         in_specs=[vmem, vmem, vmem, vmem, hbm, vmem, hbm, hbm, hbm],
         out_specs=(vmem, vmem),
         scratch_shapes=[
-            V((256, 512), BF16), V((512, 256), BF16), V((256, 640), BF16), V((256, 256), BF16),
+            V((8, 32, 512), BF16), V((512, 256), BF16), V((8, 32, 640), BF16), V((256, 256), BF16),
             V((3, 3, 4, 2, 4, 16, 512), BF16), V((8, 8, 128), F32), V((4, 2, 4, 32, 512), BF16),
             V((512, 256), BF16), V((512, 256), BF16), V((512, 256), BF16), V((512, 128), BF16),
-            V((384, 256), F32), V((1024, 128), BF16), V((128, 1024), BF16),
+            V((2, 384, 256), F32), V((1024, 128), BF16), V((128, 1024), BF16),
             V((128, 1024), BF16), V((1024, 128), BF16), V((80, 1024), BF16), V((128, LATENTS), BF16),
             V((1024, LB), F32), V((1024, LB), F32),
             V((4, 64, 512), BF16), V((4, 1, 512), F32), V((4, 64, 512), BF16), V((4, 1, 512), F32),
             V((64, 512), BF16), V((4, 1, 128), F32), V((16, 16, 128), BF16), V((16, 1, 128), F32),
-            dma((4,)), dma, dma, dma, dma, dma, dma, dma, dma, dma, dma,
-            dma((4,)), dma((4,)), dma((4,)), dma((4,)), dma((4,)), dma((4,)),
+            dma((4,)), dma, dma, dma, dma, dma, dma,
+            dma((5,)), dma((5,)), dma((5,)), dma((5,)), dma((5,)), dma((5,)),
             dma, dma, dma, dma, regular, regular, regular,
             dma, dma, dma, dma, dma, dma, dma, dma, dma, dma((4,)), dma, dma,
         ],

time: 67.9 us -> 68.6 us (1.010)
  no operation moved by 1% of the time
where the time goes in v9:
time: 68.6 us; the launch traced here: 67.4 us
  Pallas kernels  66.1 us (96%)
  between operations  1.29 us (2%)
    pallas_call x1, Pallas kernels, on_device(): pl.pallas_call(kernel, out_shape=(jax.ShapeDtypeStruct((64, 1024), BF16),...  64.3 us
    pallas_call x1, Pallas kernels, on_device(): pl.pallas_call(hand_on, out_shape=tuple((jax.ShapeDtypeStruct(r.shape, r....  1.78 us

profile of v9, /device:TPU:6, one launch (start us, length us, event | category | flops | bytes accessed | tf_op | source)
XLA Modules:
  0.0 67.4 jit_solution(14241648898621353157)
XLA Ops:
  1.3 64.3 %encoder.1 = (bf16[64,1024]{1,0:T(8,128)(2,1)}, bf16[64,2048]{1,0:T(8,128)(2,1)}) custom-call(s32[1,3]{1,0:T(1,128)} %bitcast.11, s32[1,1]{1,0:T(1,128)} %bitcast.6.valid_ref, bf16[32,1024]{1,0:T(8,128)(2,1)} %rec_ref.1, bf16[32,512]{1,0:T(8,128)(2,1)} %bitcast.10, bf16[3,3,4,16,512]{4,3,2,1,0:T(8,128)(2,1)} %bitcast.7, f32[3,64]{1,0:T(4,128)} %cb_ref.1, ...), custom_call_target="tpu_custom_call" | custom-call | tf_op jit(solution)/shard_map/encoder/pallas_call | solution.py:498
  65.6 1.8 %hand_on.1 = (bf16[64,1024]{1,0:T(8,128)(2,1)}, bf16[64,2048]{1,0:T(8,128)(2,1)}) custom-call(bf16[64,1024]{1,0:T(8,128)(2,1)} %get-tuple-element.4.feat, bf16[64,2048]{1,0:T(8,128)(2,1)} %get-tuple-element.5.att), custom_call_target="tpu_custom_call" | custom-call | tf_op jit(solution)/shard_map/hand_on/pallas_call | solution.py:528

commit v10 on v8

--- a/solution.py
+++ b/solution.py
@@ -342,8 +342,6 @@
     for g in range(4):
         sent(g)
     drain(kv_r, kvall.at[:, 0:896])
-    for copy in feature_copies:
-        copy.start()
     ka[0:64, :] = (kvall[0:64, :].astype(F32) * 0.125).astype(BF16)
     va[0:64, :] = kvall[64:128, :]
     kt[...] = jnp.transpose(ka[...].astype(F32)).astype(BF16)
@@ -397,6 +395,8 @@
             out = term if out is None else out + term
         return out / total, peak + jnp.log(total)
 
+    for copy in feature_copies:
+        copy.start()
     drain(xr, xrecv.at[1:4])
     drain(xlr, xlse.at[1:4])
     for b in range(4):
@@ -426,16 +426,10 @@
                 recv_sem=zlr, device_id=device, device_id_type=MESH),
         )
 
-    def far_first(n):
-        k = (n + 1) // 2
-        return 8 + k * (1 - 2 * lax.rem(n, 2))
-
-    def z_start(n, carry):
-        for copy in z_copies(far_first(n)):
+    far_first = [8, 7, 9, 6, 10, 5, 11, 4, 12, 3, 13, 2, 14, 1, 15]
+    for i in far_first:
+        for copy in z_copies(i):
             copy.start()
-        return carry
-
-    lax.fori_loop(0, NZ - 1, z_start, 0)
     my_rows, my_lanes, my_b = tile_of(z)
     zrecv[0] = zsend[my_rows, my_lanes]
     zlse[0] = zlse_send[my_b]
@@ -464,11 +458,8 @@
         for i in range(1, NX):
             remote(strip, strip, bs, br, at_x(i)).start()
 
-    def a_start(n, carry):
-        a_copy(far_first(n), z).start()
-        return carry
-
-    lax.fori_loop(0, NZ - 1, a_start, 0)
+    for i in far_first:
+        a_copy(i, z).start()
     for da in (0, 1, -1, 2):
         strip = zsend.at[0:16, 0 : 384 if da == 0 else 512]
         drain(ar.at[lax.rem(z // 4 + da + 4, 4)], strip)

time: 67.9 us -> 67.9 us (level)
  no operation moved by 1% of the time
where the time goes in v10:
time: 67.9 us; the launch traced here: 66.9 us
  Pallas kernels  65.6 us (97%)
  between operations  1.29 us (2%)
    pallas_call x1, Pallas kernels, on_device(): pl.pallas_call(kernel, out_shape=(jax.ShapeDtypeStruct((64, 1024), BF16),...  63.8 us
    pallas_call x1, Pallas kernels, on_device(): pl.pallas_call(hand_on, out_shape=tuple((jax.ShapeDtypeStruct(r.shape, r....  1.78 us

profile of v10, /device:TPU:6, one launch (start us, length us, event | category | flops | bytes accessed | tf_op | source)
XLA Modules:
  0.0 66.9 jit_solution(16051889755951359976)
XLA Ops:
  1.3 63.8 %encoder.1 = (bf16[64,1024]{1,0:T(8,128)(2,1)}, bf16[64,2048]{1,0:T(8,128)(2,1)}) custom-call(s32[1,3]{1,0:T(1,128)} %bitcast.11, s32[1,1]{1,0:T(1,128)} %bitcast.6.valid_ref, bf16[32,1024]{1,0:T(8,128)(2,1)} %rec_ref.1, bf16[32,512]{1,0:T(8,128)(2,1)} %bitcast.10, bf16[3,3,4,16,512]{4,3,2,1,0:T(8,128)(2,1)} %bitcast.7, f32[3,64]{1,0:T(4,128)} %cb_ref.1, ...), custom_call_target="tpu_custom_call" | custom-call | tf_op jit(solution)/shard_map/encoder/pallas_call | solution.py:490
  65.1 1.8 %hand_on.1 = (bf16[64,1024]{1,0:T(8,128)(2,1)}, bf16[64,2048]{1,0:T(8,128)(2,1)}) custom-call(bf16[64,1024]{1,0:T(8,128)(2,1)} %get-tuple-element.4.feat, bf16[64,2048]{1,0:T(8,128)(2,1)} %get-tuple-element.5.att), custom_call_target="tpu_custom_call" | custom-call | tf_op jit(solution)/shard_map/hand_on/pallas_call | solution.py:520
